TPU v7x, 1024 devices: a whole 4x8x16 slice. The times are simulated.
1024 devices in a mesh: dom: 128 (over x, z, core), sub: 8 (over y).
Axes of the slice: x: 4, y: 8, z: 16, core: 2. Of those that a mesh axis runs over, the one named last changes fastest.
Arguments:
- solution: float32 [20, 9, 131072], P(None, None, ('dom', 'sub')), may hold values from -6 to 6
- geometry: float32 [7, 131072], P(None, ('dom', 'sub')), may hold values from 0.5 to 2
- cluster: int32 [131072], P(('dom', 'sub')), may hold values from 0 to 1, as said below
- neighbour: int32 [4, 131072], P(None, ('dom', 'sub')), may hold values from 0 to 255, as said below
- orient: int32 [4, 131072], P(None, ('dom', 'sub')), may hold values from 0 to 11
- send_elem: int32 [4, 32768], P(None, ('dom', 'sub')), may hold values from 0 to 127
- stiff_time: float32 [3, 20, 20], replicated, may hold values from -1.25 to 1.25
- stiff_vol: float32 [3, 20, 20], replicated, may hold values from -1.25 to 1.25
- jacobians: float32 [3, 9, 9], replicated, may hold values from -2 to 2
- flux_minus: float32 [4, 9, 9], replicated, may hold values from -2 to 2
- flux_plus: float32 [4, 9, 9], replicated, may hold values from -2 to 2
- lifting: float32 [4, 20, 10], replicated, may hold values from -2 to 2
- restrict: float32 [4, 10, 20], replicated, may hold values from -1.25 to 1.25
- orient_mat: float32 [3, 10, 10], replicated, may hold values from -2 to 2
Outputs:
- advanced: float32 [20, 9, 131072], P(None, None, ('dom', 'sub'))
Inputs may be any that keep to these rules, and one draw needn't show every extreme that they name: `neighbour`: values below 128 are this device's elements; 128 + d * 32 + s names slot s received from direction d (0: the device one lower along dom, 1: one higher along dom, 2: one lower along sub, 3: one higher along sub). On each device every slot of a direction in which a device exists is named by exactly one face, and no slot of a direction without a device is named. On each device the elements of cluster 0 come first, at most 64 of them, and some device holds exactly 64.
All inputs are finite; a program needn't handle non-finite values.
Results may differ from a plain program's by a relative error of at most 0.0001.
Values sent between devices are 32-bit elements; how exact they have to be, the bound alone decides.
A program may use at most 32 MiB of HBM per device.

v0:
```python
import jax
import jax.numpy as jnp
from jax import lax
from jax.sharding import PartitionSpec as P

step_length = 0.4


def shifted(block, axis, distance):
    devices = range(lax.axis_size(axis))
    route = [(i - distance, i) for i in devices if i - distance in devices]
    return lax.ppermute(block, axis, route)


def predict(values, scales, stiff_time, jacobians, spans):
    highest = lax.Precision.HIGHEST
    current = values
    sums = [(end_time - begin_time) * values for begin_time, end_time in spans]
    factorial = 1.0
    for degree in range(1, 4):
        summed = jnp.zeros(values.shape, jnp.float32)
        for dim_id in range(3):
            inner_sum = jnp.einsum("bc,cqe->bqe", stiff_time[dim_id], current, precision=highest)
            summed = summed + scales[dim_id] * jnp.einsum(
                "bqe,qr->bre", inner_sum, jacobians[dim_id], precision=highest
            )
        current = -summed
        factorial = factorial * (degree + 1)
        sums = [
            partial_sum
            + (end_time ** (degree + 1) - begin_time ** (degree + 1)) / factorial * current
            for partial_sum, (begin_time, end_time) in zip(sums, spans)
        ]
    return sums


def correct(
    own_part,
    sources,
    rows,
    orient,
    geometry,
    stiff_vol,
    jacobians,
    flux_minus,
    flux_plus,
    lifting,
    restrict,
    orient_mat,
):
    highest = lax.Precision.HIGHEST
    elements = own_part.shape[2]
    columns = sources.shape[2]
    traces = jnp.einsum("jbc,cqm->bqjm", restrict, sources, precision=highest)
    own_traces = traces[:, :, :, :elements]
    trace_flat = traces.reshape(traces.shape[0] * traces.shape[1], 4 * columns)
    positions = orient // 3 * columns + rows
    gathered = jnp.take(trace_flat, positions, axis=1).reshape(
        traces.shape[0], traces.shape[1], 4, elements
    )
    rotation = orient % 3
    turned = jnp.zeros(gathered.shape, jnp.float32)
    for turn_id in range(3):
        rotated = jnp.einsum("ab,bqfe->aqfe", orient_mat[turn_id], gathered, precision=highest)
        turned = turned + jnp.where(rotation[None, None] == turn_id, rotated, 0.0)
    volume = jnp.zeros(own_part.shape, jnp.float32)
    for dim_id in range(3):
        inner_sum = jnp.einsum("bc,cqe->bqe", stiff_vol[dim_id], own_part, precision=highest)
        volume = volume + geometry[dim_id] * jnp.einsum(
            "bqe,qr->bre", inner_sum, jacobians[dim_id], precision=highest
        )
    flux_sum = jnp.zeros(own_part.shape, jnp.float32)
    for face_id in range(4):
        local_term = jnp.einsum(
            "cb,bqe->cqe", lifting[face_id], own_traces[:, :, face_id], precision=highest
        )
        neighbour_term = jnp.einsum(
            "cb,bqe->cqe", lifting[face_id], turned[:, :, face_id], precision=highest
        )
        riemann = jnp.einsum("cqe,qr->cre", local_term, flux_minus[face_id], precision=highest)
        riemann = riemann + jnp.einsum(
            "cqe,qr->cre", neighbour_term, flux_plus[face_id], precision=highest
        )
        flux_sum = flux_sum + geometry[3 + face_id] * riemann
    return volume - flux_sum


def trade_faces(values, send_elem):
    outgoing = [jnp.take(values, send_elem[slot_dir], axis=1) for slot_dir in range(4)]
    lower_dom = shifted(outgoing[0], "dom", 1)
    upper_dom = shifted(outgoing[1], "dom", -1)
    lower_sub = shifted(outgoing[2], "sub", 1)
    upper_sub = shifted(outgoing[3], "sub", -1)
    return jnp.concatenate([lower_dom, upper_dom, lower_sub, upper_sub], axis=1)


def local(
    solution,
    geometry,
    cluster,
    neighbour,
    orient,
    send_elem,
    stiff_time,
    stiff_vol,
    jacobians,
    flux_minus,
    flux_plus,
    lifting,
    restrict,
    orient_mat,
):
    basis_count = solution.shape[0]
    quant_count = solution.shape[1]
    elements = solution.shape[2]
    flat_rows = basis_count * quant_count
    matrices = (stiff_vol, jacobians, flux_minus, flux_plus, lifting, restrict, orient_mat)
    first_part, late_part = predict(
        solution,
        geometry,
        stiff_time,
        jacobians,
        [(0.0, step_length), (step_length, 2.0 * step_length)],
    )
    arrived = trade_faces(first_part.reshape(flat_rows, elements), send_elem)
    ghosts_first = arrived.reshape(basis_count, quant_count, arrived.shape[1])
    sources_one = jnp.concatenate([first_part, ghosts_first], axis=2)
    change_one = correct(first_part, sources_one, neighbour, orient, geometry, *matrices)
    halfway = solution + change_one
    fine_part = predict(halfway, geometry, stiff_time, jacobians, [(0.0, step_length)])[0]
    second_part = jnp.where(cluster[None, None] == 0, fine_part, late_part)
    received = trade_faces(second_part.reshape(flat_rows, elements), send_elem)
    ghosts_second = received.reshape(basis_count, quant_count, received.shape[1])
    sources_two = jnp.concatenate([second_part, ghosts_second], axis=2)
    change_two = correct(second_part, sources_two, neighbour, orient, geometry, *matrices)
    return halfway + change_two


def solution(mesh):
    return jax.shard_map(
        local,
        mesh=mesh,
        in_specs=(
            P(None, None, ("dom", "sub")),
            P(None, ("dom", "sub")),
            P(("dom", "sub")),
            P(None, ("dom", "sub")),
            P(None, ("dom", "sub")),
            P(None, ("dom", "sub")),
            P(),
            P(),
            P(),
            P(),
            P(),
            P(),
            P(),
            P(),
        ),
        out_specs=P(None, None, ("dom", "sub")),
        check_vma=False,
    )
```

profile of v0, /device:TPU:30, one launch (start us, length us, event | category | flops | bytes accessed | tf_op | source)
XLA Modules:
  0.0 91.1 jit_solution(5193582424820560627)
XLA Ops:
  0.0 1.2 %fusion.228 = f32[20,9,128]{2,0,1:T(8,128)S(1)} fusion(f32[20,9,128]{2,0,1:T(8,128)} %param.18, f32[3,20,20]{2,1,0:T(8,128)} %param.24), kind=kOutput, calls=%fused_computation.309 | convolution fusion | flops 5529600 | bytes 215040 | tf_op jit(solution)/shard_map/bc,cqe->bqe/dot_general | solution.py:23
  1.8 0.4 copy-done.9
  2.9 0.3 fusion.9
  4.1 0.3 convolution_multiply_fusion.19
  4.5 0.3 convolution_multiply_fusion.18
  4.8 0.3 fusion.13
  6.0 0.3 convolution_multiply_fusion.16
  6.3 0.3 convolution_multiply_fusion.15
  6.7 0.4 fusion.67
  7.2 0.6 copy-done.10
  7.8 0.6 gather_fusion
  8.5 1.9 %collective-permute-start = (f32[180,32]{0,1:T(8,128)S(1)}, f32[180,32]{0,1:T(8,128)S(1)}, u32[]{:S(2)}, u32[]{:S(2)}) collective-permute-start(f32[180,32]{0,1:T(8,128)S(1)} %select_bitcast_fusion.7), channel_id=1, source_target_pairs={{0,8},{8,16},{16,24},{24,32},{32,40},{40,48},{48,56},{56,64},{64,7... | collective-permute-start | bytes 69128 | tf_op jit(solution)/shard_map/ppermute | solution.py:12
  10.4 0.6 gather_fusion.1
  11.1 17.9 %collective-permute-start.1 = (f32[180,32]{0,1:T(8,128)S(1)}, f32[180,32]{0,1:T(8,128)S(1)}, u32[]{:S(2)}, u32[]{:S(2)}) collective-permute-start(f32[180,32]{0,1:T(8,128)S(1)} %select_bitcast_fusion.6), channel_id=1, source_target_pairs={{8,0},{16,8},{24,16},{32,24},{40,32},{48,40},{56,48},{64,56},{72,6... | collective-permute-start | bytes 69128 | tf_op jit(solution)/shard_map/ppermute | solution.py:12
  29.0 0.6 gather_fusion.2
  29.7 4.7 %collective-permute-start.2 = (f32[180,32]{0,1:T(8,128)S(1)}, f32[180,32]{0,1:T(8,128)S(1)}, u32[]{:S(2)}, u32[]{:S(2)}) collective-permute-start(f32[180,32]{0,1:T(8,128)S(1)} %select_bitcast_fusion.5), channel_id=1, source_target_pairs={{0,1},{1,2},{2,3},{3,4},{4,5},{5,6},{6,7},{8,9},{9,10},{10,11},{11... | collective-permute-start | bytes 69128 | tf_op jit(solution)/shard_map/ppermute | solution.py:12
  34.4 0.6 gather_fusion.3
  35.1 2.1 %collective-permute-start.3 = (f32[180,32]{0,1:T(8,128)S(1)}, f32[180,32]{0,1:T(8,128)S(1)}, u32[]{:S(2)}, u32[]{:S(2)}) collective-permute-start(f32[180,32]{0,1:T(8,128)S(1)} %select_bitcast_fusion.4), channel_id=1, source_target_pairs={{1,0},{2,1},{3,2},{4,3},{5,4},{6,5},{7,6},{9,8},{10,9},{11,10},{12... | collective-permute-start | bytes 69128 | tf_op jit(solution)/shard_map/ppermute | solution.py:12
  38.0 0.4 copy-done.7
  38.5 0.7 copy-done.4
  39.2 0.7 copy-done.5
  39.9 0.7 copy-done.6
  40.7 0.3 convolution_multiply_fusion.12
  41.0 0.3 convolution_multiply_fusion.13
  42.3 0.7 copy-done.2
  43.0 0.7 convolution_bitcast_fusion.1
  44.3 1.0 %gather_fusion.4 = f32[512,90]{1,0:T(8,128)S(1)} fusion(f32[90,1024]{0,1:T(8,128)S(1)} %copy.113, s32[1024]{0:T(1024)S(1)} %pad_clamp_fusion), kind=kCustom, calls=%fused_computation.1.clone | custom fusion | bytes 370688 | tf_op jit(solution)/shard_map/jit(_take)/gather | solution.py:58
  45.8 0.4 convolution_select_fusion.5
  46.2 0.4 fusion.5
  46.6 0.4 fusion.4
  49.8 0.3 fusion.95
  50.5 0.3 fusion.26
  50.9 0.3 fusion.27
  51.2 0.3 fusion.28
  51.6 0.4 fusion.25
  51.9 0.4 fusion.21
  53.1 0.3 convolution_multiply_fusion.10
  53.5 0.3 convolution_multiply_fusion.9
  53.8 0.3 fusion.32
  55.0 0.3 convolution_multiply_fusion.7
  55.3 0.3 convolution_multiply_fusion.6
  55.7 0.3 fusion.36
  56.9 0.3 convolution_multiply_fusion.4
  57.5 0.4 fusion.43
  58.1 0.6 gather_fusion.5
  58.7 0.6 gather_fusion.6
  59.3 0.6 gather_fusion.7
  59.9 0.6 gather_fusion.8
  61.1 1.9 %collective-permute-start.4 = (f32[180,32]{0,1:T(8,128)S(1)}, f32[180,32]{0,1:T(8,128)S(1)}, u32[]{:S(2)}, u32[]{:S(2)}) collective-permute-start(f32[180,32]{0,1:T(8,128)S(1)} %select_bitcast_fusion.3), channel_id=1, source_target_pairs={{0,8},{8,16},{16,24},{24,32},{32,40},{40,48},{48,56},{56,64},{64,7... | collective-permute-start | bytes 69128 | tf_op jit(solution)/shard_map/ppermute | solution.py:12
  63.1 5.7 %collective-permute-start.5 = (f32[180,32]{0,1:T(8,128)S(1)}, f32[180,32]{0,1:T(8,128)S(1)}, u32[]{:S(2)}, u32[]{:S(2)}) collective-permute-start(f32[180,32]{0,1:T(8,128)S(1)} %select_bitcast_fusion.2), channel_id=1, source_target_pairs={{8,0},{16,8},{24,16},{32,24},{40,32},{48,40},{56,48},{64,56},{72,6... | collective-permute-start | bytes 69128 | tf_op jit(solution)/shard_map/ppermute | solution.py:12
  68.9 4.8 %collective-permute-start.6 = (f32[180,32]{0,1:T(8,128)S(1)}, f32[180,32]{0,1:T(8,128)S(1)}, u32[]{:S(2)}, u32[]{:S(2)}) collective-permute-start(f32[180,32]{0,1:T(8,128)S(1)} %select_bitcast_fusion.1), channel_id=1, source_target_pairs={{0,1},{1,2},{2,3},{3,4},{4,5},{5,6},{6,7},{8,9},{9,10},{10,11},{11... | collective-permute-start | bytes 69128 | tf_op jit(solution)/shard_map/ppermute | solution.py:12
  73.9 2.1 %collective-permute-start.7 = (f32[180,32]{0,1:T(8,128)S(1)}, f32[180,32]{0,1:T(8,128)S(1)}, u32[]{:S(2)}, u32[]{:S(2)}) collective-permute-start(f32[180,32]{0,1:T(8,128)S(1)} %select_bitcast_fusion), channel_id=1, source_target_pairs={{1,0},{2,1},{3,2},{4,3},{5,4},{6,5},{7,6},{9,8},{10,9},{11,10},{12... | collective-permute-start | bytes 69128 | tf_op jit(solution)/shard_map/ppermute | solution.py:12
  76.0 0.3 convolution_multiply_fusion
  77.0 3.9 %collective-permute-done.7 = f32[180,32]{0,1:T(8,128)S(1)} collective-permute-done((f32[180,32]{0,1:T(8,128)S(1)}, f32[180,32]{0,1:T(8,128)S(1)}, u32[]{:S(2)}, u32[]{:S(2)}) %collective-permute-start.7) | collective-permute-done | bytes 23072 | tf_op jit(solution)/shard_map/ppermute | solution.py:12
  81.0 0.7 convolution_bitcast_fusion
  82.7 1.0 %gather_fusion.9 = f32[512,90]{1,0:T(8,128)S(1)} fusion(f32[90,1024]{0,1:T(8,128)S(1)} %copy.160, s32[1024]{0:T(1024)S(1)} %pad_clamp_fusion), kind=kCustom, calls=%fused_computation.9.clone | custom fusion | bytes 370688 | tf_op jit(solution)/shard_map/jit(_take)/gather | solution.py:58
  83.9 0.4 convolution_select_fusion.2
  84.3 0.4 fusion.2
  84.7 0.4 fusion.1
  89.0 0.3 fusion.54
  89.3 0.3 fusion.55
  89.6 0.4 fusion.52
  90.0 0.4 fusion.48
  90.4 0.7 copy.172
  (125 shorter events, 18.4 us)
Async XLA Ops:
  0.0 1.2 %copy-start = (f32[20,9,128]{2,0,1:T(8,128)S(1)}, f32[20,9,128]{2,0,1:T(8,128)}, u32[]{:S(2)}) copy-start(f32[20,9,128]{2,0,1:T(8,128)} %param.18) | copy-start | bytes 276484
  0.0 1.2 %copy-start.1 = (f32[3,20,20]{2,1,0:T(8,128)S(1)}, f32[3,20,20]{2,1,0:T(8,128)}, u32[]{:S(2)}) copy-start(f32[3,20,20]{2,1,0:T(8,128)} %param.24) | copy-start | bytes 14404
  1.5 0.7 copy-start.9
  1.5 0.7 copy-start.8
  7.1 0.7 copy-start.10
  8.5 33.3 %collective-permute-start = (f32[180,32]{0,1:T(8,128)S(1)}, f32[180,32]{0,1:T(8,128)S(1)}, u32[]{:S(2)}, u32[]{:S(2)}) collective-permute-start(f32[180,32]{0,1:T(8,128)S(1)} %select_bitcast_fusion.7), channel_id=1, source_target_pairs={{0,8},{8,16},{16,24},{24,32},{32,40},{40,48},{48,56},{56,64},{64,7... | collective-permute-start | bytes 69128 | tf_op jit(solution)/shard_map/ppermute | solution.py:12
  11.1 30.7 %collective-permute-start.1 = (f32[180,32]{0,1:T(8,128)S(1)}, f32[180,32]{0,1:T(8,128)S(1)}, u32[]{:S(2)}, u32[]{:S(2)}) collective-permute-start(f32[180,32]{0,1:T(8,128)S(1)} %select_bitcast_fusion.6), channel_id=1, source_target_pairs={{8,0},{16,8},{24,16},{32,24},{40,32},{48,40},{56,48},{64,56},{72,6... | collective-permute-start | bytes 69128 | tf_op jit(solution)/shard_map/ppermute | solution.py:12
  29.7 12.1 %collective-permute-start.2 = (f32[180,32]{0,1:T(8,128)S(1)}, f32[180,32]{0,1:T(8,128)S(1)}, u32[]{:S(2)}, u32[]{:S(2)}) collective-permute-start(f32[180,32]{0,1:T(8,128)S(1)} %select_bitcast_fusion.5), channel_id=1, source_target_pairs={{0,1},{1,2},{2,3},{3,4},{4,5},{5,6},{6,7},{8,9},{9,10},{10,11},{11... | collective-permute-start | bytes 69128 | tf_op jit(solution)/shard_map/ppermute | solution.py:12
  35.0 2.2 %copy-start.3 = (f32[3,20,20]{2,1,0:T(8,128)S(1)}, f32[3,20,20]{2,1,0:T(8,128)}, u32[]{:S(2)}) copy-start(f32[3,20,20]{2,1,0:T(8,128)} %param.25) | copy-start | bytes 14404
  35.1 7.0 %collective-permute-start.3 = (f32[180,32]{0,1:T(8,128)S(1)}, f32[180,32]{0,1:T(8,128)S(1)}, u32[]{:S(2)}, u32[]{:S(2)}) collective-permute-start(f32[180,32]{0,1:T(8,128)S(1)} %select_bitcast_fusion.4), channel_id=1, source_target_pairs={{1,0},{2,1},{3,2},{4,3},{5,4},{6,5},{7,6},{9,8},{10,9},{11,10},{12... | collective-permute-start | bytes 69128 | tf_op jit(solution)/shard_map/ppermute | solution.py:12
  37.7 0.7 copy-start.7
  38.5 0.7 copy-start.4
  39.2 0.7 copy-start.5
  39.9 0.7 copy-start.6
  41.0 0.7 copy-start.13
  41.0 0.7 copy-start.11
  41.0 0.7 copy-start.12
  42.2 0.7 copy-start.2
  61.1 15.8 %collective-permute-start.4 = (f32[180,32]{0,1:T(8,128)S(1)}, f32[180,32]{0,1:T(8,128)S(1)}, u32[]{:S(2)}, u32[]{:S(2)}) collective-permute-start(f32[180,32]{0,1:T(8,128)S(1)} %select_bitcast_fusion.3), channel_id=1, source_target_pairs={{0,8},{8,16},{16,24},{24,32},{32,40},{40,48},{48,56},{56,64},{64,7... | collective-permute-start | bytes 69128 | tf_op jit(solution)/shard_map/ppermute | solution.py:12
  63.1 13.8 %collective-permute-start.5 = (f32[180,32]{0,1:T(8,128)S(1)}, f32[180,32]{0,1:T(8,128)S(1)}, u32[]{:S(2)}, u32[]{:S(2)}) collective-permute-start(f32[180,32]{0,1:T(8,128)S(1)} %select_bitcast_fusion.2), channel_id=1, source_target_pairs={{8,0},{16,8},{24,16},{32,24},{40,32},{48,40},{56,48},{64,56},{72,6... | collective-permute-start | bytes 69128 | tf_op jit(solution)/shard_map/ppermute | solution.py:12
  68.9 8.0 %collective-permute-start.6 = (f32[180,32]{0,1:T(8,128)S(1)}, f32[180,32]{0,1:T(8,128)S(1)}, u32[]{:S(2)}, u32[]{:S(2)}) collective-permute-start(f32[180,32]{0,1:T(8,128)S(1)} %select_bitcast_fusion.1), channel_id=1, source_target_pairs={{0,1},{1,2},{2,3},{3,4},{4,5},{5,6},{6,7},{8,9},{9,10},{10,11},{11... | collective-permute-start | bytes 69128 | tf_op jit(solution)/shard_map/ppermute | solution.py:12
  73.9 7.0 %collective-permute-start.7 = (f32[180,32]{0,1:T(8,128)S(1)}, f32[180,32]{0,1:T(8,128)S(1)}, u32[]{:S(2)}, u32[]{:S(2)}) collective-permute-start(f32[180,32]{0,1:T(8,128)S(1)} %select_bitcast_fusion), channel_id=1, source_target_pairs={{1,0},{2,1},{3,2},{4,3},{5,4},{6,5},{7,6},{9,8},{10,9},{11,10},{12... | collective-permute-start | bytes 69128 | tf_op jit(solution)/shard_map/ppermute | solution.py:12
where the time goes:
time: 91.8 us; the launch traced here: 91.1 us
  starting transfers between devices  41.2 us (45%)
  matrix products  29.5 us (32%)
  local copies, waits for them, and re-layouts  14.2 us (15%)
  waiting for transfers between devices  4.2 us (5%)
  between operations  1.15 us (1%)
    ppermute x8, starting transfers between devices, shifted(): return lax.ppermute(block, axis, route)  41.2 us
    dot_general x18, matrix products, predict(): jnp.einsum('bqe,qr->bre', inner_sum, jacobians[dim_id], precision=highest)  6.21 us
    dot_general x18, matrix products, predict(): jnp.einsum('bc,cqe->bqe', stiff_time[dim_id], current, precision=highest)  5.68 us
    unnamed x32, local copies, waits for them, and re-layouts  4.93 us
    gather x8, local copies, waits for them, and re-layouts, trade_faces(): jnp.take(values, send_elem[slot_dir], axis=1)  4.82 us
    ppermute x8, waiting for transfers between devices, shifted(): return lax.ppermute(block, axis, route)  4.2 us
    dot_general x8, matrix products, correct(): jnp.einsum('cqe,qr->cre', neighbour_term, flux_plus[face_id], precision=h...  2.75 us
    dot_general x8, matrix products, correct(): jnp.einsum('cqe,qr->cre', local_term, flux_minus[face_id], precision=high...  2.68 us
  transfers between devices with their start and end apart: 8, of which 2 were waited for; matrix products, arithmetic and copies ran while one was open for 5% of the time, Pallas kernels for 0%

commit v1 on v0

v1 whole, which is shorter than its diff:
```python
import functools
import jax
import jax.numpy as jnp
from jax import lax
from jax.experimental import pallas as pl
from jax.experimental.pallas import tpu as pltpu
from jax.sharding import PartitionSpec as P

STEP = 0.4
BASIS = 20
QUANT = 9
ROWS = 192
LANES = 256
TRACE = 96
ELEMS = 128
SLOTS = 32
MESH = pl.DeviceIdType.MESH
F32 = jnp.float32
BF16 = jnp.bfloat16


def nn(a, b):
    return lax.dot_general(a, b, (((1,), (0,)), ((), ())), preferred_element_type=F32)


def nt(a, b):
    return lax.dot_general(a, b, (((1,), (1,)), ((), ())), preferred_element_type=F32)


def exact(a, b):
    return lax.dot_general(
        a, b, (((1,), (0,)), ((), ())), precision=lax.Precision.HIGHEST, preferred_element_type=F32
    )


def split(x):
    hi = x.astype(BF16)
    return hi, (x - hi.astype(F32)).astype(BF16)


def wide(x):
    return jnp.concatenate(split(x), axis=1)


def tall(x):
    return jnp.concatenate(split(x), axis=0)


def onehot(mask):
    return jnp.where(mask, 1.0, 0.0).astype(BF16)


def iota(shape, dim):
    return lax.broadcasted_iota(jnp.int32, shape, dim)


def spread(x, places):
    hi, lo = split(x)
    return nn(hi, places) + nn(lo, places)


def lift_rows(rows, x):
    hi, lo = split(x)
    return nn(rows, hi) + nn(rows, lo)


def fold(product):
    half = product.shape[0] // 2
    top, bottom = product[:half], product[half:]
    return top[:, :ELEMS] + (top[:, ELEMS:] + bottom[:, :ELEMS])


def nine(index):
    return (index * 57) >> 9


def kernel(
    x_any, geo_any, clu_any, nb_any, ori_any, snd_any, st_any, sv_any, jac_any, fm_any, fp_any,
    lif_any, res_any, om_any, out_ref,
    x_in, geo_in, clu_in, nb_in, ori_in, snd_in, st_in, sv_in, jac_in, fm_in, fp_in, lif_in,
    res_in, om_in,
    x_ref, time_mat, vol_mat, own_mat, far_mat, trace_mat, near_hot, outgoing, ghosts,
    in_sem, send_sem, recv_sem,
):
    pairs = [
        (x_any, x_in), (st_any, st_in), (jac_any, jac_in), (geo_any, geo_in), (snd_any, snd_in),
        (res_any, res_in), (nb_any, nb_in), (ori_any, ori_in), (sv_any, sv_in), (fm_any, fm_in),
        (lif_any, lif_in), (om_any, om_in), (fp_any, fp_in), (clu_any, clu_in),
    ]
    loads = []
    for place, (source, target) in enumerate(pairs):
        load = pltpu.make_async_copy(source, target, in_sem.at[place])
        load.start()
        loads.append(load)

    dom, sub = lax.axis_index("dom"), lax.axis_index("sub")
    doms, subs = lax.axis_size("dom"), lax.axis_size("sub")
    dom_up, dom_down = lax.rem(dom + 1, doms), lax.rem(dom + doms - 1, doms)
    sub_up, sub_down = lax.rem(sub + 1, subs), lax.rem(sub + subs - 1, subs)
    targets = [(dom_up, sub), (dom_down, sub), (dom, sub_up), (dom, sub_down)]
    barrier = pltpu.get_barrier_semaphore()
    for target in targets:
        pl.semaphore_signal(barrier, inc=1, device_id=target, device_id_type=MESH)

    row = iota((ROWS, 32), 0)
    in_rows = row < BASIS * QUANT
    row_b = nine(row)
    row_q = row - QUANT * row_b
    basis_rows = onehot((row_b == iota((ROWS, 32), 1)) & in_rows)[:, :BASIS]
    quant_rows = onehot((row_q == iota((ROWS, 32), 1)) & in_rows)[:, :QUANT]
    col = iota((BASIS, LANES), 1)
    in_cols = col < BASIS * QUANT
    col_b = nine(col)
    col_q = col - QUANT * col_b
    basis_cols = onehot((col_b == iota((BASIS, LANES), 0)) & in_cols)
    quant_cols = onehot((col_q == iota((BASIS, LANES), 0)) & in_cols)[:QUANT]

    loads[1].wait()
    loads[2].wait()
    factors = jnp.concatenate([spread(jac_in[d].T, quant_cols) for d in range(3)], axis=1)
    jac_wide = lift_rows(quant_rows, factors)
    stiff = jnp.concatenate([spread(st_in[d], basis_cols) for d in range(3)], axis=1)
    time_mat[...] = tall(lift_rows(basis_rows, stiff) * jac_wide)

    loads[0].wait()
    for b in range(BASIS):
        x_ref[pl.ds(QUANT * b, QUANT), :] = x_in[b]
    x_ref[pl.ds(BASIS * QUANT, ROWS - BASIS * QUANT), :] = jnp.zeros(
        (ROWS - BASIS * QUANT, ELEMS), F32
    )
    loads[3].wait()
    blank = jnp.zeros((LANES - ROWS, 2 * ELEMS), BF16)

    def stacked(values, first, count):
        parts = []
        for g in range(first, first + count):
            parts += [wide(geo_in[pl.ds(g, 1), :] * values), blank]
        return jnp.concatenate(parts, axis=0)

    def predict(values, spans):
        current = values
        sums = [(b - a) * values for a, b in spans]
        factorial = 1.0
        for degree in range(1, 4):
            current = fold(nn(time_mat[...], stacked(current, 0, 3)))
            factorial = factorial * (degree + 1)
            sign = -1.0 if degree % 2 else 1.0
            sums = [
                s + (sign * (b ** (degree + 1) - a ** (degree + 1)) / factorial) * current
                for s, (a, b) in zip(sums, spans)
            ]
        return sums

    first_part, late_part = predict(x_ref[...], [(0.0, STEP), (STEP, 2.0 * STEP)])

    loads[4].wait()
    eye = onehot(iota((SLOTS, SLOTS), 0) == iota((SLOTS, SLOTS), 1))
    named = nt(eye, snd_in[...].astype(F32).astype(BF16))
    elem = iota((SLOTS, ELEMS), 1)
    picks = jnp.concatenate(
        [onehot(named[:, d : d + 1].astype(jnp.int32) == elem) for d in range(4)], axis=0
    )
    pick_both = jnp.concatenate([picks, picks], axis=1)

    def send(turn, values):
        outgoing[turn, :, pl.ds(0, ROWS)] = nt(pick_both, wide(values))
        if turn == 0:
            pl.semaphore_wait(barrier, 4)
        copies = []
        for d in range(4):
            part = pl.ds(SLOTS * d, SLOTS)
            copy = pltpu.make_async_remote_copy(
                src_ref=outgoing.at[turn, part],
                dst_ref=ghosts.at[turn, part],
                send_sem=send_sem.at[turn, d],
                recv_sem=recv_sem.at[turn, d],
                device_id=targets[d],
                device_id_type=MESH,
            )
            copy.start()
            copies.append(copy)
        return copies

    copies_one = send(0, first_part)

    loads[5].wait()
    face_row = iota((TRACE, 16), 0)
    face_b = nine(face_row)
    face_rows = onehot((face_b == iota((TRACE, 16), 1)) & (face_row < 90))[:, :10]
    same_row = iota((TRACE, ROWS), 0)
    same_col = iota((TRACE, ROWS), 1)
    same = (same_row - QUANT * nine(same_row)) == (same_col - QUANT * nine(same_col))
    trace_blocks = []
    for j in range(4):
        block = lift_rows(face_rows, spread(res_in[j], basis_cols[:, :ROWS]))
        trace_blocks.append(jnp.where(same, block, 0.0))
    trace_mat[...] = tall(jnp.concatenate(trace_blocks, axis=0))

    loads[6].wait()
    loads[7].wait()
    facing = (ori_in[...] * 11) >> 5
    turning = ori_in[...] - 3 * facing
    behind = nb_in[...]
    near_key = jnp.where(behind < ELEMS, behind + ELEMS * facing, -1)
    key_row = iota((4 * ELEMS, ELEMS), 0)
    for f in range(4):
        near_hot[:, pl.ds(ELEMS * f, ELEMS)] = onehot(key_row == near_key[f : f + 1])

    slot_row = iota((ELEMS, ELEMS), 0) + ELEMS
    info_row = iota((16, ELEMS), 0)
    slot_info = jnp.zeros((16, ELEMS), F32)
    slot_hot = jnp.zeros((ELEMS, ELEMS), F32)
    for f in range(4):
        hot = jnp.where(slot_row == behind[f : f + 1], 1.0, 0.0)
        slot_hot = slot_hot + hot
        scale = geo_in[pl.ds(3 + f, 1), :]
        scale_hi = scale.astype(BF16).astype(F32)
        scale_mid = (scale - scale_hi).astype(BF16).astype(F32)
        scale_low = scale - scale_hi - scale_mid
        info = jnp.where(info_row == 0, facing[f : f + 1].astype(F32), 0.0)
        info = jnp.where(info_row == 1, (4 * turning[f : f + 1] + f).astype(F32), info)
        info = jnp.where(info_row == 2, scale_hi, info)
        info = jnp.where(info_row == 3, scale_mid, info)
        info = jnp.where(info_row == 4, scale_low, info)
        slot_info = slot_info + nt(info.astype(BF16), hot.astype(BF16))
    slot_hot = slot_hot.astype(BF16)
    slot_both = jnp.concatenate([slot_hot, slot_hot], axis=0)
    slot_face = slot_info[0:1]
    slot_kind = slot_info[1:2]
    slot_scale = slot_info[2:3] + slot_info[3:4] + slot_info[4:5]

    def mask_of(lanes):
        piece = jnp.broadcast_to(jnp.where(lanes, 1.0, 0.0), (16, ELEMS)).astype(BF16)
        piece = jnp.concatenate([piece] * (TRACE // 16), axis=0)
        return jnp.concatenate([piece, piece], axis=1)

    loads[8].wait()
    stiff = jnp.concatenate([spread(sv_in[d], basis_cols) for d in range(3)], axis=1)
    vol_mat[...] = tall(lift_rows(basis_rows, stiff) * jac_wide)
    loads[9].wait()
    loads[10].wait()
    fluxes = jnp.concatenate([spread(-fm_in[f].T, quant_cols) for f in range(4)], axis=1)
    lifted = jnp.concatenate(
        [spread(exact(lif_in[f], res_in[f]), basis_cols) for f in range(4)], axis=1
    )
    own_mat[...] = tall(lift_rows(basis_rows, lifted) * lift_rows(quant_rows, fluxes))

    loads[11].wait()
    loads[12].wait()
    far_col = iota((16, 4 * TRACE), 1)
    far_face = (far_col * 683) >> 16
    far_rem = far_col - TRACE * far_face
    far_b = nine(far_rem)
    far_q = far_rem - QUANT * far_b
    far_in = far_rem < 90
    far_row = iota((16, 4 * TRACE), 0)
    far_basis = (far_b == far_row) & far_in
    far_basis_hot = onehot(far_basis)[:10]
    lifted_far = []
    for h in range(3):
        turned = spread(om_in[h], far_basis_hot)
        total = jnp.zeros((BASIS, 4 * TRACE), F32)
        for f in range(4):
            hi, lo = split(jnp.where(far_face[:10] == f, turned, 0.0))
            lift_hi, lift_lo = split(lif_in[f])
            total = total + (nn(lift_hi, hi) + nn(lift_hi, lo) + nn(lift_lo, hi))
        lifted_far.append(total)
    lifted_far = jnp.concatenate(lifted_far, axis=1)
    flux_far = jnp.zeros((QUANT, 4 * TRACE), F32)
    for f in range(4):
        places = onehot((far_q == far_row) & far_in & (far_face == f))[:QUANT]
        flux_far = flux_far + spread(-fp_in[f].T, places)
    flux_far = lift_rows(quant_rows, flux_far)
    flux_far = jnp.concatenate([flux_far] * 3, axis=1)
    far_mat[...] = tall(lift_rows(basis_rows, lifted_far) * flux_far)

    near_masks = [[mask_of(turning[f : f + 1] == h) for f in range(4)] for h in range(3)]
    slot_masks = [[mask_of(slot_kind == 4.0 * h + f) for f in range(4)] for h in range(3)]

    def correct_near(values):
        change = fold(nn(vol_mat[...], stacked(values, 0, 3)))
        change = change + fold(nn(own_mat[...], stacked(values, 3, 4)))
        traces = fold(nn(trace_mat[...], wide(values)))
        sources = jnp.concatenate(
            [traces[TRACE * j : TRACE * (j + 1)] for j in range(4)], axis=1
        )
        picked = nn(tall(sources), near_hot[...])
        picked = picked[:TRACE] + picked[TRACE:]
        scaled = [
            wide(geo_in[pl.ds(3 + f, 1), :] * picked[:, ELEMS * f : ELEMS * (f + 1)])
            for f in range(4)
        ]
        parts = [scaled[f] * near_masks[h][f] for h in range(3) for f in range(4)]
        return change + fold(nn(far_mat[...], jnp.concatenate(parts, axis=0)))

    def correct_far(turn):
        slots = ghosts[turn, :, pl.ds(0, ROWS)]
        traces = fold(nt(trace_mat[...], tall(slots)))
        chosen = traces[:TRACE]
        for j in range(1, 4):
            chosen = jnp.where(slot_face == j, traces[TRACE * j : TRACE * (j + 1)], chosen)
        scaled = wide(slot_scale * chosen)
        parts = [scaled * slot_masks[h][f] for h in range(3) for f in range(4)]
        lifted = fold(nn(far_mat[...], jnp.concatenate(parts, axis=0)))
        return nn(wide(lifted), slot_both)

    def finish(copies):
        for copy in copies:
            copy.wait_recv()

    near_one = x_ref[...] + correct_near(first_part)
    finish(copies_one)
    halfway = near_one + correct_far(0)
    fine_part = predict(halfway, [(0.0, STEP)])[0]
    loads[13].wait()
    second_part = jnp.where(clu_in[...] == 0, fine_part, late_part)
    copies_two = send(1, second_part)
    near_two = halfway + correct_near(second_part)
    finish(copies_two)
    out_ref[...] = (near_two + correct_far(1))[: BASIS * QUANT]
    for copy in copies_one + copies_two:
        copy.wait_send()


def local(solution, geometry, cluster, *others):
    args = (solution, geometry, cluster.reshape(1, ELEMS), *others)
    held = [pltpu.VMEM(a.shape, a.dtype) for a in args]
    result = pl.pallas_call(
        kernel,
        out_shape=jax.ShapeDtypeStruct((BASIS * QUANT, ELEMS), F32),
        in_specs=[pl.BlockSpec(memory_space=pl.ANY)] * len(args),
        out_specs=pl.BlockSpec(memory_space=pltpu.VMEM),
        scratch_shapes=held
        + [
            pltpu.VMEM((ROWS, ELEMS), F32),
            pltpu.VMEM((2 * ROWS, 3 * LANES), BF16),
            pltpu.VMEM((2 * ROWS, 3 * LANES), BF16),
            pltpu.VMEM((2 * ROWS, 4 * LANES), BF16),
            pltpu.VMEM((2 * ROWS, 12 * TRACE), BF16),
            pltpu.VMEM((8 * TRACE, ROWS), BF16),
            pltpu.VMEM((4 * ELEMS, 4 * ELEMS), BF16),
            pltpu.VMEM((2, ELEMS, LANES), F32),
            pltpu.VMEM((2, ELEMS, LANES), F32),
            pltpu.SemaphoreType.DMA((len(args),)),
            pltpu.SemaphoreType.DMA((2, 4)),
            pltpu.SemaphoreType.DMA((2, 4)),
        ],
        compiler_params=pltpu.CompilerParams(
            collective_id=0, has_side_effects=True, vmem_limit_bytes=32 * 1024 * 1024
        ),
    )(*args)
    return result.reshape(solution.shape)


def solution(mesh):
    split_last = P(None, ("dom", "sub"))
    return jax.shard_map(
        local,
        mesh=mesh,
        in_specs=(P(None, None, ("dom", "sub")), split_last, P(("dom", "sub")))
        + (split_last,) * 3
        + (P(),) * 8,
        out_specs=P(None, None, ("dom", "sub")),
        check_vma=False,
    )
```

time: 91.8 us -> 37.3 us (0.41)
  the two profiles are of different devices: /device:TPU:30 before, /device:TPU:24 now
where the time goes in v1:
time: 37.3 us; the launch traced here: 37 us
  Pallas kernels  33.1 us (89%)
  local copies, waits for them, and re-layouts  3.77 us (10%)
    pallas_call x1, Pallas kernels, local(): pl.pallas_call(kernel, out_shape=jax.ShapeDtypeStruct((BASIS * QUANT, ELE...  33.1 us
    unnamed x33, local copies, waits for them, and re-layouts  3.08 us

profile of v1, /device:TPU:24, one launch (start us, length us, event | category | flops | bytes accessed | tf_op | source)
XLA Modules:
  0.0 37.0 jit_solution(5017978815688592792)
XLA Ops:
  0.0 0.0 copy-start.8
  0.0 0.7 %copy.24.jac_any = f32[3,9,9]{2,1,0:T(8,128)S(1)} copy(f32[3,9,9]{2,0,1:T(4,128)} %param.22) | data formatting | bytes 1944 | tf_op args[8]
  0.7 0.0 copy-done.8
  0.7 0.0 copy-start.11
  0.7 0.0 copy-start.12
  0.7 0.0 copy-start.9
  0.8 0.7 %copy-done.11 = f32[4,9,9]{2,0,1:T(4,128)S(1)} copy-done((f32[4,9,9]{2,0,1:T(4,128)S(1)}, f32[4,9,9]{2,0,1:T(4,128)}, u32[]{:S(2)}) %copy-start.11) | copy-done | bytes 1320
  1.5 0.0 copy-start.7
  1.5 0.0 copy-done.12
  1.5 0.0 copy-done.9
  1.5 0.0 copy-start.10
  1.5 0.7 %copy-done.10 = f32[4,20,10]{1,0,2:T(4,128)S(1)} copy-done((f32[4,20,10]{1,0,2:T(4,128)S(1)}, f32[4,20,10]{1,0,2:T(4,128)}, u32[]{:S(2)}) %copy-start.10) | copy-done | bytes 3224
  2.3 0.1 copy.27.lif_any
  2.4 0.0 copy-done.7
  2.4 0.0 copy-start
  2.4 0.0 copy-start.1
  2.4 0.0 copy-start.2
  2.4 0.0 copy-start.3
  2.4 0.0 copy-start.4
  2.4 0.0 copy-start.5
  2.5 0.0 copy-start.6
  2.5 0.7 %copy-done = f32[3,20,20]{2,1,0:T(8,128)S(1)} copy-done((f32[3,20,20]{2,1,0:T(8,128)S(1)}, f32[3,20,20]{2,1,0:T(8,128)}, u32[]{:S(2)}) %copy-start) | copy-done | bytes 4824
  3.2 0.0 copy-done.1
  3.2 0.0 copy-done.2
  3.2 0.0 copy-done.3
  3.2 0.0 copy-done.4
  3.2 0.0 copy-done.5
  3.2 0.0 copy-done.6
  3.2 33.1 %shard_map.136 = f32[180,128]{1,0:T(8,128)S(1)} custom-call(f32[20,9,128]{2,1,0:T(8,128)S(1)} %copy.23.x_any, f32[7,128]{1,0:T(8,128)S(1)} %copy-done.2, s32[1,128]{1,0:T(1,128)S(1)} %bitcast.1, s32[4,128]{1,0:T(4,128)S(1)} %copy-done.3, s32[4,128]{1,0:T(4,128)S(1)} %copy-done.4, s32[4,32]{1,0:T(4,128)S(1)} %copy-done.5, f32[3,20,20]{2,1,0:T(8,128)S(1)} %copy-done, ...), custom_call_target="tpu_custom_call" | custom-call | tf_op jit(solution)/shard_map/pallas_call | solution.py:328
  36.3 0.7 %copy.30 = f32[20,9,128]{2,0,1:T(8,128)} copy(f32[20,9,128]{2,1,0:T(8,128)S(1)} %reshape.7) | data formatting | bytes 184320 | tf_op jit(solution)/shard_map/reshape | solution.py:352
  (6 shorter events, 0.1 us)
Async XLA Ops:
  0.0 0.7 %copy-start.8 = (f32[3,10,10]{2,0,1:T(4,128)S(1)}, f32[3,10,10]{2,0,1:T(4,128)}, u32[]{:S(2)}) copy-start(f32[3,10,10]{2,0,1:T(4,128)} %param.27) | copy-start | bytes 3604
  0.7 0.7 %copy-start.11 = (f32[4,9,9]{2,0,1:T(4,128)S(1)}, f32[4,9,9]{2,0,1:T(4,128)}, u32[]{:S(2)}) copy-start(f32[4,9,9]{2,0,1:T(4,128)} %param.23) | copy-start | bytes 3892
  0.7 0.7 %copy-start.12 = (f32[4,9,9]{2,0,1:T(4,128)S(1)}, f32[4,9,9]{2,0,1:T(4,128)}, u32[]{:S(2)}) copy-start(f32[4,9,9]{2,0,1:T(4,128)} %param.24) | copy-start | bytes 3892
  0.7 0.8 %copy-start.9 = (f32[4,10,20]{2,0,1:T(4,128)S(1)}, f32[4,10,20]{2,0,1:T(4,128)}, u32[]{:S(2)}) copy-start(f32[4,10,20]{2,0,1:T(4,128)} %param.26) | copy-start | bytes 9604
  1.5 0.9 %copy-start.7 = (f32[20,9,128]{2,0,1:T(8,128)S(1)}, f32[20,9,128]{2,0,1:T(8,128)}, u32[]{:S(2)}) copy-start(f32[20,9,128]{2,0,1:T(8,128)} %param.14) | copy-start | bytes 276484
  1.5 0.8 %copy-start.10 = (f32[4,20,10]{1,0,2:T(4,128)S(1)}, f32[4,20,10]{1,0,2:T(4,128)}, u32[]{:S(2)}) copy-start(f32[4,20,10]{1,0,2:T(4,128)} %param.25) | copy-start | bytes 9604
  2.4 0.8 %copy-start = (f32[3,20,20]{2,1,0:T(8,128)S(1)}, f32[3,20,20]{2,1,0:T(8,128)}, u32[]{:S(2)}) copy-start(f32[3,20,20]{2,1,0:T(8,128)} %st_any.1) | copy-start | bytes 14404
  2.4 0.8 %copy-start.1 = (f32[3,20,20]{2,1,0:T(8,128)S(1)}, f32[3,20,20]{2,1,0:T(8,128)}, u32[]{:S(2)}) copy-start(f32[3,20,20]{2,1,0:T(8,128)} %sv_any.1) | copy-start | bytes 14404
  2.4 0.8 %copy-start.2 = (f32[7,128]{1,0:T(8,128)S(1)}, f32[7,128]{1,0:T(8,128)}, u32[]{:S(2)}) copy-start(f32[7,128]{1,0:T(8,128)} %geo_any.1) | copy-start | bytes 10756
  2.4 0.8 %copy-start.3 = (s32[4,128]{1,0:T(4,128)S(1)}, s32[4,128]{1,0:T(4,128)}, u32[]{:S(2)}) copy-start(s32[4,128]{1,0:T(4,128)} %nb_any.1) | copy-start | bytes 6148
  2.4 0.8 %copy-start.4 = (s32[4,128]{1,0:T(4,128)S(1)}, s32[4,128]{1,0:T(4,128)}, u32[]{:S(2)}) copy-start(s32[4,128]{1,0:T(4,128)} %ori_any.1) | copy-start | bytes 6148
  2.4 0.7 %copy-start.5 = (s32[4,32]{1,0:T(4,128)S(1)}, s32[4,32]{1,0:T(4,128)}, u32[]{:S(2)}) copy-start(s32[4,32]{1,0:T(4,128)} %snd_any.1) | copy-start | bytes 1540
  2.5 0.7 %copy-start.6 = (s32[128]{0:T(128)S(1)}, s32[128]{0:T(128)}, u32[]{:S(2)}) copy-start(s32[128]{0:T(128)} %param.16) | copy-start | bytes 1540

commit v2 on v1

--- a/solution.py
+++ b/solution.py
@@ -70,8 +70,12 @@
     return top[:, :ELEMS] + (top[:, ELEMS:] + bottom[:, :ELEMS])
 
 
-def nine(index):
-    return (index * 57) >> 9
+def by_basis(index):
+    return (index * 205) >> 12
+
+
+def by_face_basis(index):
+    return (index * 205) >> 11
 
 
 def kernel(
@@ -104,27 +108,27 @@
 
     row = iota((ROWS, 32), 0)
     in_rows = row < BASIS * QUANT
-    row_b = nine(row)
-    row_q = row - QUANT * row_b
+    row_q = by_basis(row)
+    row_b = row - BASIS * row_q
     basis_rows = onehot((row_b == iota((ROWS, 32), 1)) & in_rows)[:, :BASIS]
     quant_rows = onehot((row_q == iota((ROWS, 32), 1)) & in_rows)[:, :QUANT]
     col = iota((BASIS, LANES), 1)
     in_cols = col < BASIS * QUANT
-    col_b = nine(col)
-    col_q = col - QUANT * col_b
+    col_q = by_basis(col)
+    col_b = col - BASIS * col_q
     basis_cols = onehot((col_b == iota((BASIS, LANES), 0)) & in_cols)
     quant_cols = onehot((col_q == iota((BASIS, LANES), 0)) & in_cols)[:QUANT]
 
     loads[1].wait()
     loads[2].wait()
-    factors = jnp.concatenate([spread(jac_in[d].T, quant_cols) for d in range(3)], axis=1)
+    factors = jnp.concatenate([spread(jac_in[:, d, :].T, quant_cols) for d in range(3)], axis=1)
     jac_wide = lift_rows(quant_rows, factors)
     stiff = jnp.concatenate([spread(st_in[d], basis_cols) for d in range(3)], axis=1)
     time_mat[...] = tall(lift_rows(basis_rows, stiff) * jac_wide)
 
     loads[0].wait()
-    for b in range(BASIS):
-        x_ref[pl.ds(QUANT * b, QUANT), :] = x_in[b]
+    for q in range(QUANT):
+        x_ref[pl.ds(BASIS * q, BASIS), :] = x_in[q]
     x_ref[pl.ds(BASIS * QUANT, ROWS - BASIS * QUANT), :] = jnp.zeros(
         (ROWS - BASIS * QUANT, ELEMS), F32
     )
@@ -185,14 +189,14 @@
 
     loads[5].wait()
     face_row = iota((TRACE, 16), 0)
-    face_b = nine(face_row)
+    face_b = face_row - 10 * by_face_basis(face_row)
     face_rows = onehot((face_b == iota((TRACE, 16), 1)) & (face_row < 90))[:, :10]
     same_row = iota((TRACE, ROWS), 0)
     same_col = iota((TRACE, ROWS), 1)
-    same = (same_row - QUANT * nine(same_row)) == (same_col - QUANT * nine(same_col))
+    same = by_face_basis(same_row) == by_basis(same_col)
     trace_blocks = []
     for j in range(4):
-        block = lift_rows(face_rows, spread(res_in[j], basis_cols[:, :ROWS]))
+        block = lift_rows(face_rows, spread(res_in[:, j, :], basis_cols[:, :ROWS]))
         trace_blocks.append(jnp.where(same, block, 0.0))
     trace_mat[...] = tall(jnp.concatenate(trace_blocks, axis=0))
 
@@ -239,9 +243,9 @@
     vol_mat[...] = tall(lift_rows(basis_rows, stiff) * jac_wide)
     loads[9].wait()
     loads[10].wait()
-    fluxes = jnp.concatenate([spread(-fm_in[f].T, quant_cols) for f in range(4)], axis=1)
+    fluxes = jnp.concatenate([spread(-fm_in[:, f, :].T, quant_cols) for f in range(4)], axis=1)
     lifted = jnp.concatenate(
-        [spread(exact(lif_in[f], res_in[f]), basis_cols) for f in range(4)], axis=1
+        [spread(exact(lif_in[:, f, :].T, res_in[:, f, :]), basis_cols) for f in range(4)], axis=1
     )
     own_mat[...] = tall(lift_rows(basis_rows, lifted) * lift_rows(quant_rows, fluxes))
 
@@ -250,26 +254,26 @@
     far_col = iota((16, 4 * TRACE), 1)
     far_face = (far_col * 683) >> 16
     far_rem = far_col - TRACE * far_face
-    far_b = nine(far_rem)
-    far_q = far_rem - QUANT * far_b
+    far_q = by_face_basis(far_rem)
+    far_b = far_rem - 10 * far_q
     far_in = far_rem < 90
     far_row = iota((16, 4 * TRACE), 0)
     far_basis = (far_b == far_row) & far_in
     far_basis_hot = onehot(far_basis)[:10]
     lifted_far = []
     for h in range(3):
-        turned = spread(om_in[h], far_basis_hot)
+        turned = spread(om_in[:, h, :], far_basis_hot)
         total = jnp.zeros((BASIS, 4 * TRACE), F32)
         for f in range(4):
             hi, lo = split(jnp.where(far_face[:10] == f, turned, 0.0))
-            lift_hi, lift_lo = split(lif_in[f])
+            lift_hi, lift_lo = split(lif_in[:, f, :].T)
             total = total + (nn(lift_hi, hi) + nn(lift_hi, lo) + nn(lift_lo, hi))
         lifted_far.append(total)
     lifted_far = jnp.concatenate(lifted_far, axis=1)
     flux_far = jnp.zeros((QUANT, 4 * TRACE), F32)
     for f in range(4):
         places = onehot((far_q == far_row) & far_in & (far_face == f))[:QUANT]
-        flux_far = flux_far + spread(-fp_in[f].T, places)
+        flux_far = flux_far + spread(-fp_in[:, f, :].T, places)
     flux_far = lift_rows(quant_rows, flux_far)
     flux_far = jnp.concatenate([flux_far] * 3, axis=1)
     far_mat[...] = tall(lift_rows(basis_rows, lifted_far) * flux_far)
@@ -317,17 +321,28 @@
     copies_two = send(1, second_part)
     near_two = halfway + correct_near(second_part)
     finish(copies_two)
-    out_ref[...] = (near_two + correct_far(1))[: BASIS * QUANT]
+    x_ref[...] = near_two + correct_far(1)
+    for q in range(QUANT):
+        out_ref[q] = x_ref[pl.ds(BASIS * q, BASIS), :]
     for copy in copies_one + copies_two:
         copy.wait_send()
 
 
-def local(solution, geometry, cluster, *others):
-    args = (solution, geometry, cluster.reshape(1, ELEMS), *others)
+def local(
+    solution, geometry, cluster, neighbour, orient, send_elem, stiff_time, stiff_vol, jacobians,
+    flux_minus, flux_plus, lifting, restrict, orient_mat,
+):
+    inner = (1, 0, 2)
+    args = (
+        solution.transpose(inner), geometry, cluster.reshape(1, ELEMS), neighbour, orient,
+        send_elem, stiff_time, stiff_vol, jacobians.transpose(inner),
+        flux_minus.transpose(inner), flux_plus.transpose(inner), lifting.transpose(2, 0, 1),
+        restrict.transpose(inner), orient_mat.transpose(inner),
+    )
     held = [pltpu.VMEM(a.shape, a.dtype) for a in args]
     result = pl.pallas_call(
         kernel,
-        out_shape=jax.ShapeDtypeStruct((BASIS * QUANT, ELEMS), F32),
+        out_shape=jax.ShapeDtypeStruct((QUANT, BASIS, ELEMS), F32),
         in_specs=[pl.BlockSpec(memory_space=pl.ANY)] * len(args),
         out_specs=pl.BlockSpec(memory_space=pltpu.VMEM),
         scratch_shapes=held
@@ -346,10 +361,10 @@
             pltpu.SemaphoreType.DMA((2, 4)),
         ],
         compiler_params=pltpu.CompilerParams(
-            collective_id=0, has_side_effects=True, vmem_limit_bytes=32 * 1024 * 1024
+            collective_id=0, has_side_effects=True, vmem_limit_bytes=60 * 1024 * 1024
         ),
     )(*args)
-    return result.reshape(solution.shape)
+    return result.transpose(inner)
 
 
 def solution(mesh):

time: 37.3 us -> 35.6 us (0.954)
  the two profiles are of different devices: /device:TPU:24 before, /device:TPU:56 now
where the time goes in v2:
time: 35.6 us; the launch traced here: 35.4 us
  Pallas kernels  33.9 us (95%)
  local copies, waits for them, and re-layouts  1.55 us (4%)
    pallas_call x1, Pallas kernels, local(): pl.pallas_call(kernel, out_shape=jax.ShapeDtypeStruct((QUANT, BASIS, ELEM...  33.9 us
    unnamed x1, local copies, waits for them, and re-layouts  1.55 us

profile of v2, /device:TPU:56, one launch (start us, length us, event | category | flops | bytes accessed | tf_op | source)
XLA Modules:
  0.0 35.4 jit_solution(6884242847595562541)
XLA Ops:
  0.0 33.9 %shard_map.136 = f32[9,20,128]{2,1,0:T(8,128)} custom-call(f32[9,20,128]{2,1,0:T(8,128)} %bitcast.10, f32[7,128]{1,0:T(8,128)} %geo_any.1, s32[1,128]{1,0:T(1,128)} %bitcast.17, s32[4,128]{1,0:T(4,128)} %nb_any.1, s32[4,128]{1,0:T(4,128)} %ori_any.1, s32[4,32]{1,0:T(4,128)} %snd_any.1, f32[3,20,20]{2,1,0:T(8,128)} %st_any.1, f32[3,20,20]{2,1,0:T(8,128)} %sv_any.1, ...), custom_call_target="tpu_custom_call" | custom-call | tf_op jit(solution)/shard_map/pallas_call | solution.py:343
  33.9 1.5 %copy.16 = f32[20,9,128]{2,0,1:T(8,128)} copy(f32[20,9,128]{2,0,1:T(8,128)} %bitcast.9) | data formatting | bytes 184320

commit v3 on v2

v3 whole, which is shorter than its diff:
```python
import functools
import jax
import jax.numpy as jnp
from jax import lax
from jax.experimental import pallas as pl
from jax.experimental.pallas import tpu as pltpu
from jax.sharding import PartitionSpec as P

STEP = 0.4
BASIS = 20
QUANT = 9
ROWS = 192
LANES = 256
TRACE = 96
ELEMS = 128
SLOTS = 32
MESH = pl.DeviceIdType.MESH
F32 = jnp.float32
BF16 = jnp.bfloat16


def nn(a, b):
    return lax.dot_general(a, b, (((1,), (0,)), ((), ())), preferred_element_type=F32)


def nt(a, b):
    return lax.dot_general(a, b, (((1,), (1,)), ((), ())), preferred_element_type=F32)


def split(x):
    hi = x.astype(BF16)
    return hi, (x - hi.astype(F32)).astype(BF16)


def wide(x):
    return jnp.concatenate(split(x), axis=1)


def tall(x):
    return jnp.concatenate(split(x), axis=0)


def onehot(mask):
    return jnp.where(mask, 1.0, 0.0).astype(BF16)


def iota(shape, dim):
    return lax.broadcasted_iota(jnp.int32, shape, dim)


def triple(x):
    hi, lo = split(x)
    return jnp.concatenate([hi, lo, hi], axis=1)


def stack(pairs):
    his = [hi for hi, _ in pairs]
    return jnp.concatenate(his + his + [lo for _, lo in pairs], axis=0)


def spread(x, places):
    hi, lo = split(x)
    return nn(hi, places) + nn(lo, places)


def triple_product(x, y):
    x_hi, x_lo = split(x)
    y_hi, y_lo = split(y)
    return nn(x_hi, y_hi) + (nn(x_hi, y_lo) + nn(x_lo, y_hi))


def kron(held, left, right):
    wide_part = pl.ds(0, left.shape[1])
    for q in range(QUANT):
        held[pl.ds(BASIS * q, BASIS), wide_part] = left * right[q : q + 1]
    held[pl.ds(BASIS * QUANT, ROWS - BASIS * QUANT), wide_part] = jnp.zeros(
        (ROWS - BASIS * QUANT, left.shape[1]), F32
    )
    return held[:, wide_part]


def by_basis(index):
    return (index * 205) >> 12


def by_face_basis(index):
    return (index * 205) >> 11


def kernel(
    x_any, geo_any, clu_any, nb_any, ori_any, snd_any, st_any, sv_any, jac_any, fm_any, fp_any,
    lif_any, res_any, om_any, out_ref,
    x_in, geo_in, clu_in, nb_in, ori_in, snd_in, st_in, sv_in, jac_in, fm_in, fp_in, lif_in,
    res_in, om_in,
    x_ref, time_held, vol_held, own_held, far_held, trace_held, time_mat, vol_mat, own_mat, far_mat,
    trace_mat, near_hot, ghost_hot, outgoing, ghosts,
    in_sem, send_sem, recv_sem,
):
    pairs = [
        (x_any, x_in), (st_any, st_in), (jac_any, jac_in), (geo_any, geo_in), (snd_any, snd_in),
        (res_any, res_in), (nb_any, nb_in), (ori_any, ori_in), (sv_any, sv_in), (fm_any, fm_in),
        (lif_any, lif_in), (om_any, om_in), (fp_any, fp_in), (clu_any, clu_in),
    ]
    loads = []
    for place, (source, target) in enumerate(pairs):
        load = pltpu.make_async_copy(source, target, in_sem.at[place])
        load.start()
        loads.append(load)

    dom, sub = lax.axis_index("dom"), lax.axis_index("sub")
    doms, subs = lax.axis_size("dom"), lax.axis_size("sub")
    dom_up, dom_down = lax.rem(dom + 1, doms), lax.rem(dom + doms - 1, doms)
    sub_up, sub_down = lax.rem(sub + 1, subs), lax.rem(sub + subs - 1, subs)
    targets = [(dom_up, sub), (dom_down, sub), (dom, sub_up), (dom, sub_down)]
    barrier = pltpu.get_barrier_semaphore()
    for target in targets:
        pl.semaphore_signal(barrier, inc=1, device_id=target, device_id_type=MESH)

    col = iota((BASIS, ROWS), 1)
    in_cols = col < BASIS * QUANT
    col_q = by_basis(col)
    col_b = col - BASIS * col_q
    basis_cols = onehot((col_b == iota((BASIS, ROWS), 0)) & in_cols)
    quant_cols = onehot((col_q == iota((BASIS, ROWS), 0)) & in_cols)[:QUANT]

    loads[1].wait()
    loads[2].wait()
    factors = jnp.concatenate([spread(jac_in[:, d, :].T, quant_cols) for d in range(3)], axis=1)
    stiff = jnp.concatenate([spread(st_in[d], basis_cols) for d in range(3)], axis=1)
    time_mat[...] = triple(kron(time_held, stiff, factors))

    loads[0].wait()
    for q in range(QUANT):
        x_ref[pl.ds(BASIS * q, BASIS), :] = x_in[q]
    x_ref[pl.ds(BASIS * QUANT, ROWS - BASIS * QUANT), :] = jnp.zeros(
        (ROWS - BASIS * QUANT, ELEMS), F32
    )
    loads[3].wait()

    def scaled_three(values):
        return stack([split(geo_in[pl.ds(g, 1), :] * values) for g in range(3)])

    def predict(values, spans):
        current = values
        sums = [(b - a) * values for a, b in spans]
        factorial = 1.0
        for degree in range(1, 4):
            current = nn(time_mat[...], scaled_three(current))
            factorial = factorial * (degree + 1)
            sign = -1.0 if degree % 2 else 1.0
            sums = [
                s + (sign * (b ** (degree + 1) - a ** (degree + 1)) / factorial) * current
                for s, (a, b) in zip(sums, spans)
            ]
        return sums

    first_part, late_part = predict(x_ref[...], [(0.0, STEP), (STEP, 2.0 * STEP)])

    loads[4].wait()
    eye = onehot(iota((SLOTS, SLOTS), 0) == iota((SLOTS, SLOTS), 1))
    named = nt(eye, snd_in[...].astype(F32).astype(BF16))
    elem = iota((SLOTS, ELEMS), 1)
    picks = jnp.concatenate(
        [onehot(named[:, d : d + 1].astype(jnp.int32) == elem) for d in range(4)], axis=0
    )
    pick_both = jnp.concatenate([picks, picks], axis=1)

    outgoing[:, :, pl.ds(ROWS, LANES - ROWS)] = jnp.zeros((2, ELEMS, LANES - ROWS), F32)

    def send(turn, values):
        outgoing[turn, :, pl.ds(0, ROWS)] = nt(pick_both, wide(values))
        if turn == 0:
            pl.semaphore_wait(barrier, 4)
        copies = []
        for d in range(4):
            part = pl.ds(SLOTS * d, SLOTS)
            copy = pltpu.make_async_remote_copy(
                src_ref=outgoing.at[turn, part],
                dst_ref=ghosts.at[turn, part],
                send_sem=send_sem.at[turn, d],
                recv_sem=recv_sem.at[turn, d],
                device_id=targets[d],
                device_id_type=MESH,
            )
            copy.start()
            copies.append(copy)
        return copies

    copies_one = send(0, first_part)

    loads[5].wait()
    trace_col = iota((10, LANES), 1)
    trace_q = by_basis(trace_col)
    for j in range(4):
        places = onehot(
            (iota((BASIS, LANES), 1) - BASIS * by_basis(iota((BASIS, LANES), 1)))
            == iota((BASIS, LANES), 0)
        )
        block = spread(res_in[:, j, :], places)
        for q in range(QUANT):
            trace_held[pl.ds(TRACE * j + 10 * q, 10), :] = jnp.where(trace_q == q, block, 0.0)
        trace_held[pl.ds(TRACE * j + 90, TRACE - 90), :] = jnp.zeros((TRACE - 90, LANES), F32)
    trace_mat[...] = triple(trace_held[...])

    loads[6].wait()
    loads[7].wait()
    facing = (ori_in[...] * 11) >> 5
    turning = ori_in[...] - 3 * facing
    behind = nb_in[...]
    near_key = jnp.where(behind < ELEMS, behind + ELEMS * facing, -1)
    key_row = iota((4 * ELEMS, ELEMS), 0)
    slot_row = iota((ELEMS, ELEMS), 0) + ELEMS
    slot_face = jnp.zeros((16, ELEMS), F32)
    for f in range(4):
        part = pl.ds(ELEMS * f, ELEMS)
        near_hot[:, part] = onehot(key_row == near_key[f : f + 1])
        hot = onehot(slot_row == behind[f : f + 1])
        ghost_hot[:, part] = hot
        face = jnp.broadcast_to(facing[f : f + 1].astype(F32), (16, ELEMS)).astype(BF16)
        slot_face = slot_face + nt(face, hot)
    slot_face = slot_face[0:1]

    loads[8].wait()
    stiff = jnp.concatenate([spread(sv_in[d], basis_cols) for d in range(3)], axis=1)
    vol_mat[...] = triple(kron(vol_held, stiff, factors))

    loads[9].wait()
    loads[10].wait()
    loads[11].wait()
    loads[12].wait()
    far_col = iota((16, TRACE), 1)
    far_q = by_face_basis(far_col)
    far_row = iota((16, TRACE), 0)
    far_in = far_col < 90
    far_basis = onehot((far_col - 10 * far_q == far_row) & far_in)[:10]
    far_quant = onehot((far_q == far_row) & far_in)[:QUANT]
    turned = jnp.concatenate([spread(om_in[:, h, :], far_basis) for h in range(3)], axis=1)
    own_left, own_right, far_left, far_right = [], [], [], []
    for f in range(4):
        lifting = lif_in[:, f, :].T
        own_left.append(spread(lifting, far_basis))
        own_right.append(spread(-fm_in[:, f, :].T, far_quant))
        far_left.append(triple_product(lifting, turned))
        far_right += [spread(-fp_in[:, f, :].T, far_quant)] * 3
    own_left, own_right = jnp.concatenate(own_left, axis=1), jnp.concatenate(own_right, axis=1)
    far_left, far_right = jnp.concatenate(far_left, axis=1), jnp.concatenate(far_right, axis=1)
    own_mat[...] = triple(kron(own_held, own_left, own_right))
    far_mat[...] = triple(kron(far_held, far_left, far_right))

    def mask_of(lanes):
        piece = jnp.broadcast_to(jnp.where(lanes, 1.0, 0.0), (16, ELEMS)).astype(BF16)
        return jnp.concatenate([piece] * (TRACE // 16), axis=0)

    masks = [[mask_of(turning[f : f + 1] == h) for h in range(3)] for f in range(4)]
    scales = [geo_in[pl.ds(3 + f, 1), :] for f in range(4)]
    blank = jnp.zeros((LANES - ROWS, ELEMS), BF16)

    def correct_near(values):
        hi, lo = split(values)
        traces = nn(
            trace_mat[...], jnp.concatenate([hi, blank, hi, blank, lo, blank], axis=0)
        )
        traces = [traces[TRACE * j : TRACE * (j + 1)] for j in range(4)]
        change = nn(vol_mat[...], scaled_three(values))
        change = change + nn(own_mat[...], stack([split(scales[f] * traces[f]) for f in range(4)]))
        picked = nn(tall(jnp.concatenate(traces, axis=1)), near_hot[...])
        return change, picked[:TRACE] + picked[TRACE:]

    def correct_far(turn, picked):
        hi, lo = split(ghosts[turn])
        traces = nt(trace_mat[...], jnp.concatenate([hi, hi, lo], axis=1))
        chosen = traces[:TRACE]
        for j in range(1, 4):
            chosen = jnp.where(slot_face == j, traces[TRACE * j : TRACE * (j + 1)], chosen)
        received = nn(tall(chosen), ghost_hot[...])
        picked = picked + (received[:TRACE] + received[TRACE:])
        pairs = []
        for f in range(4):
            hi, lo = split(scales[f] * picked[:, ELEMS * f : ELEMS * (f + 1)])
            pairs += [(hi * masks[f][h], lo * masks[f][h]) for h in range(3)]
        return nn(far_mat[...], stack(pairs))

    def finish(copies):
        for copy in copies:
            copy.wait_recv()

    change, picked = correct_near(first_part)
    near_one = x_ref[...] + change
    finish(copies_one)
    halfway = near_one + correct_far(0, picked)
    fine_part = predict(halfway, [(0.0, STEP)])[0]
    loads[13].wait()
    second_part = jnp.where(clu_in[...] == 0, fine_part, late_part)
    copies_two = send(1, second_part)
    change, picked = correct_near(second_part)
    near_two = halfway + change
    finish(copies_two)
    x_ref[...] = near_two + correct_far(1, picked)
    for q in range(QUANT):
        out_ref[q] = x_ref[pl.ds(BASIS * q, BASIS), :]
    for copy in copies_one + copies_two:
        copy.wait_send()


def local(
    solution, geometry, cluster, neighbour, orient, send_elem, stiff_time, stiff_vol, jacobians,
    flux_minus, flux_plus, lifting, restrict, orient_mat,
):
    inner = (1, 0, 2)
    args = (
        solution.transpose(inner), geometry, cluster.reshape(1, ELEMS), neighbour, orient,
        send_elem, stiff_time, stiff_vol, jacobians.transpose(inner),
        flux_minus.transpose(inner), flux_plus.transpose(inner), lifting.transpose(2, 0, 1),
        restrict.transpose(inner), orient_mat.transpose(inner),
    )
    held = [pltpu.VMEM(a.shape, a.dtype) for a in args]
    result = pl.pallas_call(
        kernel,
        out_shape=jax.ShapeDtypeStruct((QUANT, BASIS, ELEMS), F32),
        in_specs=[pl.BlockSpec(memory_space=pl.ANY)] * len(args),
        out_specs=pl.BlockSpec(memory_space=pltpu.VMEM),
        scratch_shapes=held
        + [
            pltpu.VMEM((ROWS, ELEMS), F32),
            pltpu.VMEM((ROWS, 3 * ROWS), F32),
            pltpu.VMEM((ROWS, 3 * ROWS), F32),
            pltpu.VMEM((ROWS, 4 * TRACE), F32),
            pltpu.VMEM((ROWS, 12 * TRACE), F32),
            pltpu.VMEM((4 * TRACE, LANES), F32),
            pltpu.VMEM((ROWS, 9 * ROWS), BF16),
            pltpu.VMEM((ROWS, 9 * ROWS), BF16),
            pltpu.VMEM((ROWS, 12 * TRACE), BF16),
            pltpu.VMEM((ROWS, 36 * TRACE), BF16),
            pltpu.VMEM((4 * TRACE, 3 * LANES), BF16),
            pltpu.VMEM((4 * ELEMS, 4 * ELEMS), BF16),
            pltpu.VMEM((ELEMS, 4 * ELEMS), BF16),
            pltpu.VMEM((2, ELEMS, LANES), F32),
            pltpu.VMEM((2, ELEMS, LANES), F32),
            pltpu.SemaphoreType.DMA((len(args),)),
            pltpu.SemaphoreType.DMA((2, 4)),
            pltpu.SemaphoreType.DMA((2, 4)),
        ],
        compiler_params=pltpu.CompilerParams(
            collective_id=0, has_side_effects=True, vmem_limit_bytes=60 * 1024 * 1024
        ),
    )(*args)
    return result.transpose(inner)


def solution(mesh):
    split_last = P(None, ("dom", "sub"))
    return jax.shard_map(
        local,
        mesh=mesh,
        in_specs=(P(None, None, ("dom", "sub")), split_last, P(("dom", "sub")))
        + (split_last,) * 3
        + (P(),) * 8,
        out_specs=P(None, None, ("dom", "sub")),
        check_vma=False,
    )
```

time: 35.6 us -> 34.1 us (0.958)
  the two profiles are of different devices: /device:TPU:56 before, /device:TPU:24 now
where the time goes in v3:
time: 34.1 us; the launch traced here: 33.9 us
  Pallas kernels  32.4 us (95%)
  local copies, waits for them, and re-layouts  1.55 us (5%)
    pallas_call x1, Pallas kernels, local(): pl.pallas_call(kernel, out_shape=jax.ShapeDtypeStruct((QUANT, BASIS, ELEM...  32.4 us
    unnamed x1, local copies, waits for them, and re-layouts  1.55 us

profile of v3, /device:TPU:24, one launch (start us, length us, event | category | flops | bytes accessed | tf_op | source)
XLA Modules:
  0.0 33.9 jit_solution(4894592901284056392)
XLA Ops:
  0.0 32.4 %shard_map.136 = f32[9,20,128]{2,1,0:T(8,128)} custom-call(f32[9,20,128]{2,1,0:T(8,128)} %bitcast.10, f32[7,128]{1,0:T(8,128)} %geo_any.1, s32[1,128]{1,0:T(1,128)} %bitcast.17, s32[4,128]{1,0:T(4,128)} %nb_any.1, s32[4,128]{1,0:T(4,128)} %ori_any.1, s32[4,32]{1,0:T(4,128)} %snd_any.1, f32[3,20,20]{2,1,0:T(8,128)} %st_any.1, f32[3,20,20]{2,1,0:T(8,128)} %sv_any.1, ...), custom_call_target="tpu_custom_call" | custom-call | tf_op jit(solution)/shard_map/pallas_call | solution.py:317
  32.4 1.5 %copy.16 = f32[20,9,128]{2,0,1:T(8,128)} copy(f32[20,9,128]{2,0,1:T(8,128)} %bitcast.9) | data formatting | bytes 184320

commit v4 on v3

--- a/solution.py
+++ b/solution.py
@@ -316,7 +316,7 @@
     held = [pltpu.VMEM(a.shape, a.dtype) for a in args]
     result = pl.pallas_call(
         kernel,
-        out_shape=jax.ShapeDtypeStruct((QUANT, BASIS, ELEMS), F32),
+        out_shape=pltpu.VMEM((QUANT, BASIS, ELEMS), F32),
         in_specs=[pl.BlockSpec(memory_space=pl.ANY)] * len(args),
         out_specs=pl.BlockSpec(memory_space=pltpu.VMEM),
         scratch_shapes=held
@@ -341,7 +341,7 @@
             pltpu.SemaphoreType.DMA((2, 4)),
         ],
         compiler_params=pltpu.CompilerParams(
-            collective_id=0, has_side_effects=True, vmem_limit_bytes=60 * 1024 * 1024
+            collective_id=0, has_side_effects=True, vmem_limit_bytes=55 * 1024 * 1024
         ),
     )(*args)
     return result.transpose(inner)

time: 34.1 us -> 32.6 us (0.956)
  local copies, waits for them, and re-layouts: 1.55 us -> 0.65 us
  Pallas kernels: 32.4 us -> 31.7 us
    unnamed x1, local copies, waits for them, and re-layouts: 1.55 us -> 0.65 us
    pallas_call x1, Pallas kernels: 32.4 us -> 31.7 us  [local(): pl.pallas_call(kernel, out_shape=pltpu.VMEM((QUANT, BASIS, ELEMS), F32),...]
where the time goes in v4:
time: 32.6 us; the launch traced here: 32.4 us
  Pallas kernels  31.7 us (97%)
  local copies, waits for them, and re-layouts  0.65 us (2%)
    pallas_call x1, Pallas kernels, local(): pl.pallas_call(kernel, out_shape=pltpu.VMEM((QUANT, BASIS, ELEMS), F32),...  31.7 us

profile of v4, /device:TPU:24, one launch (start us, length us, event | category | flops | bytes accessed | tf_op | source)
XLA Modules:
  0.0 32.4 jit_solution(7860798402068069817)
XLA Ops:
  0.0 31.7 %shard_map.136 = f32[9,20,128]{2,1,0:T(8,128)S(1)} custom-call(f32[9,20,128]{2,1,0:T(8,128)} %bitcast.10, f32[7,128]{1,0:T(8,128)} %geo_any.1, s32[1,128]{1,0:T(1,128)} %bitcast.17, s32[4,128]{1,0:T(4,128)} %nb_any.1, s32[4,128]{1,0:T(4,128)} %ori_any.1, s32[4,32]{1,0:T(4,128)} %snd_any.1, f32[3,20,20]{2,1,0:T(8,128)} %st_any.1, f32[3,20,20]{2,1,0:T(8,128)} %sv_any.1, ...), custom_call_target="tpu_custom_call" | custom-call | tf_op jit(solution)/shard_map/pallas_call | solution.py:317
  31.7 0.6 %copy.16 = f32[20,9,128]{2,0,1:T(8,128)} copy(f32[20,9,128]{2,0,1:T(8,128)S(1)} %bitcast.9) | data formatting | bytes 184320

commit v5 on v4

--- a/solution.py
+++ b/solution.py
@@ -112,9 +112,24 @@
     dom_up, dom_down = lax.rem(dom + 1, doms), lax.rem(dom + doms - 1, doms)
     sub_up, sub_down = lax.rem(sub + 1, subs), lax.rem(sub + subs - 1, subs)
     targets = [(dom_up, sub), (dom_down, sub), (dom, sub_up), (dom, sub_down)]
+    below, above = dom > 0, dom < doms - 1
+    sends, arrives = [above, below, None, None], [below, above, None, None]
+    ghosts[:, pl.ds(0, 2 * SLOTS), :] = jnp.zeros((2, 2 * SLOTS, LANES), F32)
+
+    def where_any(condition, action):
+        if condition is None:
+            action()
+        else:
+            pl.when(condition)(action)
+
     barrier = pltpu.get_barrier_semaphore()
-    for target in targets:
-        pl.semaphore_signal(barrier, inc=1, device_id=target, device_id_type=MESH)
+    for d in range(4):
+        where_any(
+            sends[d],
+            functools.partial(
+                pl.semaphore_signal, barrier, inc=1, device_id=targets[d], device_id_type=MESH
+            ),
+        )
 
     col = iota((BASIS, ROWS), 1)
     in_cols = col < BASIS * QUANT
@@ -170,7 +185,7 @@
     def send(turn, values):
         outgoing[turn, :, pl.ds(0, ROWS)] = nt(pick_both, wide(values))
         if turn == 0:
-            pl.semaphore_wait(barrier, 4)
+            pl.semaphore_wait(barrier, 2 + below.astype(jnp.int32) + above.astype(jnp.int32))
         copies = []
         for d in range(4):
             part = pl.ds(SLOTS * d, SLOTS)
@@ -182,7 +197,7 @@
                 device_id=targets[d],
                 device_id_type=MESH,
             )
-            copy.start()
+            where_any(sends[d], copy.start)
             copies.append(copy)
         return copies
 
@@ -281,8 +296,8 @@
         return nn(far_mat[...], stack(pairs))
 
     def finish(copies):
-        for copy in copies:
-            copy.wait_recv()
+        for d in range(4):
+            where_any(arrives[d], copies[d].wait_recv)
 
     change, picked = correct_near(first_part)
     near_one = x_ref[...] + change
@@ -298,8 +313,9 @@
     x_ref[...] = near_two + correct_far(1, picked)
     for q in range(QUANT):
         out_ref[q] = x_ref[pl.ds(BASIS * q, BASIS), :]
-    for copy in copies_one + copies_two:
-        copy.wait_send()
+    for copies in (copies_one, copies_two):
+        for d in range(4):
+            where_any(sends[d], copies[d].wait_send)
 
 
 def local(

time: 32.6 us -> 31.2 us (0.957)
  the two profiles are of different devices: /device:TPU:24 before, /device:TPU:6 now
where the time goes in v5:
time: 31.2 us; the launch traced here: 31 us
  Pallas kernels  30.4 us (97%)
  local copies, waits for them, and re-layouts  0.65 us (2%)
    pallas_call x1, Pallas kernels, local(): pl.pallas_call(kernel, out_shape=pltpu.VMEM((QUANT, BASIS, ELEMS), F32),...  30.4 us
    unnamed x1, local copies, waits for them, and re-layouts  0.65 us

profile of v5, /device:TPU:6, one launch (start us, length us, event | category | flops | bytes accessed | tf_op | source)
XLA Modules:
  0.0 31.0 jit_solution(5459176871707809862)
XLA Ops:
  0.0 30.4 %shard_map.136 = f32[9,20,128]{2,1,0:T(8,128)S(1)} custom-call(f32[9,20,128]{2,1,0:T(8,128)} %bitcast.10, f32[7,128]{1,0:T(8,128)} %geo_any.1, s32[1,128]{1,0:T(1,128)} %bitcast.17, s32[4,128]{1,0:T(4,128)} %nb_any.1, s32[4,128]{1,0:T(4,128)} %ori_any.1, s32[4,32]{1,0:T(4,128)} %snd_any.1, f32[3,20,20]{2,1,0:T(8,128)} %st_any.1, f32[3,20,20]{2,1,0:T(8,128)} %sv_any.1, ...), custom_call_target="tpu_custom_call" | custom-call | tf_op jit(solution)/shard_map/pallas_call | solution.py:333
  30.4 0.6 %copy.16 = f32[20,9,128]{2,0,1:T(8,128)} copy(f32[20,9,128]{2,0,1:T(8,128)S(1)} %bitcast.9) | data formatting | bytes 184320

commit v6 on v5

--- a/solution.py
+++ b/solution.py
@@ -112,23 +112,17 @@
     dom_up, dom_down = lax.rem(dom + 1, doms), lax.rem(dom + doms - 1, doms)
     sub_up, sub_down = lax.rem(sub + 1, subs), lax.rem(sub + subs - 1, subs)
     targets = [(dom_up, sub), (dom_down, sub), (dom, sub_up), (dom, sub_down)]
-    below, above = dom > 0, dom < doms - 1
-    sends, arrives = [above, below, None, None], [below, above, None, None]
-    ghosts[:, pl.ds(0, 2 * SLOTS), :] = jnp.zeros((2, 2 * SLOTS, LANES), F32)
-
-    def where_any(condition, action):
-        if condition is None:
-            action()
-        else:
-            pl.when(condition)(action)
+    below, above, left, right = dom > 0, dom < doms - 1, sub > 0, sub < subs - 1
+    sends, arrives = [above, below, right, left], [below, above, left, right]
+    partners = sum(exists.astype(jnp.int32) for exists in sends)
+    ghosts[...] = jnp.zeros((2, ELEMS, LANES), F32)
 
     barrier = pltpu.get_barrier_semaphore()
     for d in range(4):
-        where_any(
-            sends[d],
+        pl.when(sends[d])(
             functools.partial(
                 pl.semaphore_signal, barrier, inc=1, device_id=targets[d], device_id_type=MESH
-            ),
+            )
         )
 
     col = iota((BASIS, ROWS), 1)
@@ -185,7 +179,7 @@
     def send(turn, values):
         outgoing[turn, :, pl.ds(0, ROWS)] = nt(pick_both, wide(values))
         if turn == 0:
-            pl.semaphore_wait(barrier, 2 + below.astype(jnp.int32) + above.astype(jnp.int32))
+            pl.semaphore_wait(barrier, partners)
         copies = []
         for d in range(4):
             part = pl.ds(SLOTS * d, SLOTS)
@@ -197,7 +191,7 @@
                 device_id=targets[d],
                 device_id_type=MESH,
             )
-            where_any(sends[d], copy.start)
+            pl.when(sends[d])(copy.start)
             copies.append(copy)
         return copies
 
@@ -297,7 +291,7 @@
 
     def finish(copies):
         for d in range(4):
-            where_any(arrives[d], copies[d].wait_recv)
+            pl.when(arrives[d])(copies[d].wait_recv)
 
     change, picked = correct_near(first_part)
     near_one = x_ref[...] + change
@@ -315,7 +309,7 @@
         out_ref[q] = x_ref[pl.ds(BASIS * q, BASIS), :]
     for copies in (copies_one, copies_two):
         for d in range(4):
-            where_any(sends[d], copies[d].wait_send)
+            pl.when(sends[d])(copies[d].wait_send)
 
 
 def local(

time: 31.2 us -> 30.5 us (0.978)
  the two profiles are of different devices: /device:TPU:6 before, /device:TPU:30 now
where the time goes in v6:
time: 30.5 us; the launch traced here: 30.4 us
  Pallas kernels  29.7 us (97%)
  local copies, waits for them, and re-layouts  0.65 us (2%)
    pallas_call x1, Pallas kernels, local(): pl.pallas_call(kernel, out_shape=pltpu.VMEM((QUANT, BASIS, ELEMS), F32),...  29.7 us
    unnamed x1, local copies, waits for them, and re-layouts  0.65 us

profile of v6, /device:TPU:30, one launch (start us, length us, event | category | flops | bytes accessed | tf_op | source)
XLA Modules:
  0.0 30.4 jit_solution(6322301252890416631)
XLA Ops:
  0.0 29.7 %shard_map.136 = f32[9,20,128]{2,1,0:T(8,128)S(1)} custom-call(f32[9,20,128]{2,1,0:T(8,128)} %bitcast.10, f32[7,128]{1,0:T(8,128)} %geo_any.1, s32[1,128]{1,0:T(1,128)} %bitcast.17, s32[4,128]{1,0:T(4,128)} %nb_any.1, s32[4,128]{1,0:T(4,128)} %ori_any.1, s32[4,32]{1,0:T(4,128)} %snd_any.1, f32[3,20,20]{2,1,0:T(8,128)} %st_any.1, f32[3,20,20]{2,1,0:T(8,128)} %sv_any.1, ...), custom_call_target="tpu_custom_call" | custom-call | tf_op jit(solution)/shard_map/pallas_call | solution.py:327
  29.7 0.6 %copy.16 = f32[20,9,128]{2,0,1:T(8,128)} copy(f32[20,9,128]{2,0,1:T(8,128)S(1)} %bitcast.9) | data formatting | bytes 184320

commit v7 on v6

--- a/solution.py
+++ b/solution.py
@@ -163,9 +163,43 @@
             ]
         return sums
 
+    for place in range(4, 9):
+        loads[place].wait()
+
+    trace_col = iota((10, LANES), 1)
+    trace_q = by_basis(trace_col)
+    for j in range(4):
+        places = onehot(
+            (iota((BASIS, LANES), 1) - BASIS * by_basis(iota((BASIS, LANES), 1)))
+            == iota((BASIS, LANES), 0)
+        )
+        block = spread(res_in[:, j, :], places)
+        for q in range(QUANT):
+            trace_held[pl.ds(TRACE * j + 10 * q, 10), :] = jnp.where(trace_q == q, block, 0.0)
+        trace_held[pl.ds(TRACE * j + 90, TRACE - 90), :] = jnp.zeros((TRACE - 90, LANES), F32)
+    trace_mat[...] = triple(trace_held[...])
+
+    facing = (ori_in[...] * 11) >> 5
+    turning = ori_in[...] - 3 * facing
+    behind = nb_in[...]
+    near_key = jnp.where(behind < ELEMS, behind + ELEMS * facing, -1)
+    key_row = iota((4 * ELEMS, ELEMS), 0)
+    slot_row = iota((ELEMS, ELEMS), 0) + ELEMS
+    slot_face = jnp.zeros((16, ELEMS), F32)
+    for f in range(4):
+        part = pl.ds(ELEMS * f, ELEMS)
+        near_hot[:, part] = onehot(key_row == near_key[f : f + 1])
+        hot = onehot(slot_row == behind[f : f + 1])
+        ghost_hot[:, part] = hot
+        face = jnp.broadcast_to(facing[f : f + 1].astype(F32), (16, ELEMS)).astype(BF16)
+        slot_face = slot_face + nt(face, hot)
+    slot_face = slot_face[0:1]
+
+    stiff = jnp.concatenate([spread(sv_in[d], basis_cols) for d in range(3)], axis=1)
+    vol_mat[...] = triple(kron(vol_held, stiff, factors))
+
     first_part, late_part = predict(x_ref[...], [(0.0, STEP), (STEP, 2.0 * STEP)])
 
-    loads[4].wait()
     eye = onehot(iota((SLOTS, SLOTS), 0) == iota((SLOTS, SLOTS), 1))
     named = nt(eye, snd_in[...].astype(F32).astype(BF16))
     elem = iota((SLOTS, ELEMS), 1)
@@ -196,42 +230,6 @@
         return copies
 
     copies_one = send(0, first_part)
-
-    loads[5].wait()
-    trace_col = iota((10, LANES), 1)
-    trace_q = by_basis(trace_col)
-    for j in range(4):
-        places = onehot(
-            (iota((BASIS, LANES), 1) - BASIS * by_basis(iota((BASIS, LANES), 1)))
-            == iota((BASIS, LANES), 0)
-        )
-        block = spread(res_in[:, j, :], places)
-        for q in range(QUANT):
-            trace_held[pl.ds(TRACE * j + 10 * q, 10), :] = jnp.where(trace_q == q, block, 0.0)
-        trace_held[pl.ds(TRACE * j + 90, TRACE - 90), :] = jnp.zeros((TRACE - 90, LANES), F32)
-    trace_mat[...] = triple(trace_held[...])
-
-    loads[6].wait()
-    loads[7].wait()
-    facing = (ori_in[...] * 11) >> 5
-    turning = ori_in[...] - 3 * facing
-    behind = nb_in[...]
-    near_key = jnp.where(behind < ELEMS, behind + ELEMS * facing, -1)
-    key_row = iota((4 * ELEMS, ELEMS), 0)
-    slot_row = iota((ELEMS, ELEMS), 0) + ELEMS
-    slot_face = jnp.zeros((16, ELEMS), F32)
-    for f in range(4):
-        part = pl.ds(ELEMS * f, ELEMS)
-        near_hot[:, part] = onehot(key_row == near_key[f : f + 1])
-        hot = onehot(slot_row == behind[f : f + 1])
-        ghost_hot[:, part] = hot
-        face = jnp.broadcast_to(facing[f : f + 1].astype(F32), (16, ELEMS)).astype(BF16)
-        slot_face = slot_face + nt(face, hot)
-    slot_face = slot_face[0:1]
-
-    loads[8].wait()
-    stiff = jnp.concatenate([spread(sv_in[d], basis_cols) for d in range(3)], axis=1)
-    vol_mat[...] = triple(kron(vol_held, stiff, factors))
 
     loads[9].wait()
     loads[10].wait()

time: 30.5 us -> 30.8 us (level)
  no operation moved by 1% of the time
where the time goes in v7:
time: 30.8 us; the launch traced here: 30.6 us
  Pallas kernels  30 us (97%)
  local copies, waits for them, and re-layouts  0.65 us (2%)
    pallas_call x1, Pallas kernels, local(): pl.pallas_call(kernel, out_shape=pltpu.VMEM((QUANT, BASIS, ELEMS), F32),...  30 us
    unnamed x1, local copies, waits for them, and re-layouts  0.65 us

profile of v7, /device:TPU:30, one launch (start us, length us, event | category | flops | bytes accessed | tf_op | source)
XLA Modules:
  0.0 30.6 jit_solution(3834973500846156822)
XLA Ops:
  0.0 30.0 %shard_map.136 = f32[9,20,128]{2,1,0:T(8,128)S(1)} custom-call(f32[9,20,128]{2,1,0:T(8,128)} %bitcast.10, f32[7,128]{1,0:T(8,128)} %geo_any.1, s32[1,128]{1,0:T(1,128)} %bitcast.17, s32[4,128]{1,0:T(4,128)} %nb_any.1, s32[4,128]{1,0:T(4,128)} %ori_any.1, s32[4,32]{1,0:T(4,128)} %snd_any.1, f32[3,20,20]{2,1,0:T(8,128)} %st_any.1, f32[3,20,20]{2,1,0:T(8,128)} %sv_any.1, ...), custom_call_target="tpu_custom_call" | custom-call | tf_op jit(solution)/shard_map/pallas_call | solution.py:325
  30.0 0.6 %copy.16 = f32[20,9,128]{2,0,1:T(8,128)} copy(f32[20,9,128]{2,0,1:T(8,128)S(1)} %bitcast.9) | data formatting | bytes 184320

commit v8 on v7

--- a/solution.py
+++ b/solution.py
@@ -185,15 +185,27 @@
     near_key = jnp.where(behind < ELEMS, behind + ELEMS * facing, -1)
     key_row = iota((4 * ELEMS, ELEMS), 0)
     slot_row = iota((ELEMS, ELEMS), 0) + ELEMS
-    slot_face = jnp.zeros((16, ELEMS), F32)
+    info_row = iota((16, ELEMS), 0)
+    slot_info = jnp.zeros((16, ELEMS), F32)
+    slot_hot = jnp.zeros((ELEMS, ELEMS), F32)
     for f in range(4):
-        part = pl.ds(ELEMS * f, ELEMS)
-        near_hot[:, part] = onehot(key_row == near_key[f : f + 1])
-        hot = onehot(slot_row == behind[f : f + 1])
-        ghost_hot[:, part] = hot
-        face = jnp.broadcast_to(facing[f : f + 1].astype(F32), (16, ELEMS)).astype(BF16)
-        slot_face = slot_face + nt(face, hot)
-    slot_face = slot_face[0:1]
+        near_hot[:, pl.ds(ELEMS * f, ELEMS)] = onehot(key_row == near_key[f : f + 1])
+        hot = jnp.where(slot_row == behind[f : f + 1], 1.0, 0.0)
+        slot_hot = slot_hot + hot
+        ghost_hot[:, pl.ds(ELEMS * f, ELEMS)] = hot.astype(BF16)
+        scale = geo_in[pl.ds(3 + f, 1), :]
+        scale_hi = scale.astype(BF16).astype(F32)
+        scale_mid = (scale - scale_hi).astype(BF16).astype(F32)
+        info = jnp.where(info_row == 0, facing[f : f + 1].astype(F32), 0.0)
+        info = jnp.where(info_row == 1, (3 * f + turning[f : f + 1]).astype(F32), info)
+        info = jnp.where(info_row == 2, scale_hi, info)
+        info = jnp.where(info_row == 3, scale_mid, info)
+        info = jnp.where(info_row == 4, scale - scale_hi - scale_mid, info)
+        slot_info = slot_info + nt(info.astype(BF16), hot.astype(BF16))
+    slot_hot = slot_hot.astype(BF16)
+    slot_both = jnp.concatenate([slot_hot, slot_hot], axis=0)
+    slot_face, slot_kind = slot_info[0:1], slot_info[1:2]
+    slot_scale = slot_info[2:3] + slot_info[3:4] + slot_info[4:5]
 
     stiff = jnp.concatenate([spread(sv_in[d], basis_cols) for d in range(3)], axis=1)
     vol_mat[...] = triple(kron(vol_held, stiff, factors))
@@ -259,6 +271,7 @@
         return jnp.concatenate([piece] * (TRACE // 16), axis=0)
 
     masks = [[mask_of(turning[f : f + 1] == h) for h in range(3)] for f in range(4)]
+    slot_masks = [mask_of(slot_kind == float(kind)) for kind in range(12)]
     scales = [geo_in[pl.ds(3 + f, 1), :] for f in range(4)]
     blank = jnp.zeros((LANES - ROWS, ELEMS), BF16)
 
@@ -273,19 +286,29 @@
         picked = nn(tall(jnp.concatenate(traces, axis=1)), near_hot[...])
         return change, picked[:TRACE] + picked[TRACE:]
 
-    def correct_far(turn, picked):
+    def flux_behind(picked):
+        pairs = []
+        for f in range(4):
+            hi, lo = split(scales[f] * picked[:, ELEMS * f : ELEMS * (f + 1)])
+            pairs += [(hi * masks[f][h], lo * masks[f][h]) for h in range(3)]
+        return nn(far_mat[...], stack(pairs))
+
+    def slot_traces(turn):
         hi, lo = split(ghosts[turn])
         traces = nt(trace_mat[...], jnp.concatenate([hi, hi, lo], axis=1))
         chosen = traces[:TRACE]
         for j in range(1, 4):
             chosen = jnp.where(slot_face == j, traces[TRACE * j : TRACE * (j + 1)], chosen)
-        received = nn(tall(chosen), ghost_hot[...])
-        picked = picked + (received[:TRACE] + received[TRACE:])
-        pairs = []
-        for f in range(4):
-            hi, lo = split(scales[f] * picked[:, ELEMS * f : ELEMS * (f + 1)])
-            pairs += [(hi * masks[f][h], lo * masks[f][h]) for h in range(3)]
-        return nn(far_mat[...], stack(pairs))
+        return chosen
+
+    def correct_joined(turn, picked):
+        received = nn(tall(slot_traces(turn)), ghost_hot[...])
+        return flux_behind(picked + (received[:TRACE] + received[TRACE:]))
+
+    def correct_slots(turn):
+        hi, lo = split(slot_scale * slot_traces(turn))
+        lifted = nn(far_mat[...], stack([(hi * mask, lo * mask) for mask in slot_masks]))
+        return nn(wide(lifted), slot_both)
 
     def finish(copies):
         for d in range(4):
@@ -294,15 +317,15 @@
     change, picked = correct_near(first_part)
     near_one = x_ref[...] + change
     finish(copies_one)
-    halfway = near_one + correct_far(0, picked)
+    halfway = near_one + correct_joined(0, picked)
     fine_part = predict(halfway, [(0.0, STEP)])[0]
     loads[13].wait()
     second_part = jnp.where(clu_in[...] == 0, fine_part, late_part)
     copies_two = send(1, second_part)
     change, picked = correct_near(second_part)
-    near_two = halfway + change
+    near_two = halfway + change + flux_behind(picked)
     finish(copies_two)
-    x_ref[...] = near_two + correct_far(1, picked)
+    x_ref[...] = near_two + correct_slots(1)
     for q in range(QUANT):
         out_ref[q] = x_ref[pl.ds(BASIS * q, BASIS), :]
     for copies in (copies_one, copies_two):

time: 30.8 us -> 30.8 us (level)
  no operation moved by 1% of the time
where the time goes in v8:
time: 30.8 us; the launch traced here: 30.7 us
  Pallas kernels  30 us (97%)
  local copies, waits for them, and re-layouts  0.65 us (2%)
    pallas_call x1, Pallas kernels, local(): pl.pallas_call(kernel, out_shape=pltpu.VMEM((QUANT, BASIS, ELEMS), F32),...  30 us
    unnamed x1, local copies, waits for them, and re-layouts  0.65 us

profile of v8, /device:TPU:30, one launch (start us, length us, event | category | flops | bytes accessed | tf_op | source)
XLA Modules:
  0.0 30.7 jit_solution(13348247889175508009)
XLA Ops:
  0.0 30.0 %shard_map.136 = f32[9,20,128]{2,1,0:T(8,128)S(1)} custom-call(f32[9,20,128]{2,1,0:T(8,128)} %bitcast.10, f32[7,128]{1,0:T(8,128)} %geo_any.1, s32[1,128]{1,0:T(1,128)} %bitcast.17, s32[4,128]{1,0:T(4,128)} %nb_any.1, s32[4,128]{1,0:T(4,128)} %ori_any.1, s32[4,32]{1,0:T(4,128)} %snd_any.1, f32[3,20,20]{2,1,0:T(8,128)} %st_any.1, f32[3,20,20]{2,1,0:T(8,128)} %sv_any.1, ...), custom_call_target="tpu_custom_call" | custom-call | tf_op jit(solution)/shard_map/pallas_call | solution.py:348
  30.0 0.6 %copy.16 = f32[20,9,128]{2,0,1:T(8,128)} copy(f32[20,9,128]{2,0,1:T(8,128)S(1)} %bitcast.9) | data formatting | bytes 184320

commit v9 on v8

--- a/solution.py
+++ b/solution.py
@@ -163,7 +163,41 @@
             ]
         return sums
 
-    for place in range(4, 9):
+    first_part, late_part = predict(x_ref[...], [(0.0, STEP), (STEP, 2.0 * STEP)])
+
+    loads[4].wait()
+    eye = onehot(iota((SLOTS, SLOTS), 0) == iota((SLOTS, SLOTS), 1))
+    named = nt(eye, snd_in[...].astype(F32).astype(BF16))
+    elem = iota((SLOTS, ELEMS), 1)
+    picks = jnp.concatenate(
+        [onehot(named[:, d : d + 1].astype(jnp.int32) == elem) for d in range(4)], axis=0
+    )
+    pick_both = jnp.concatenate([picks, picks], axis=1)
+
+    outgoing[:, :, pl.ds(ROWS, LANES - ROWS)] = jnp.zeros((2, ELEMS, LANES - ROWS), F32)
+
+    def send(turn, values):
+        outgoing[turn, :, pl.ds(0, ROWS)] = nt(pick_both, wide(values))
+        if turn == 0:
+            pl.semaphore_wait(barrier, partners)
+        copies = []
+        for d in range(4):
+            part = pl.ds(SLOTS * d, SLOTS)
+            copy = pltpu.make_async_remote_copy(
+                src_ref=outgoing.at[turn, part],
+                dst_ref=ghosts.at[turn, part],
+                send_sem=send_sem.at[turn, d],
+                recv_sem=recv_sem.at[turn, d],
+                device_id=targets[d],
+                device_id_type=MESH,
+            )
+            pl.when(sends[d])(copy.start)
+            copies.append(copy)
+        return copies
+
+    copies_one = send(0, first_part)
+
+    for place in range(5, 9):
         loads[place].wait()
 
     trace_col = iota((10, LANES), 1)
@@ -209,39 +243,6 @@
 
     stiff = jnp.concatenate([spread(sv_in[d], basis_cols) for d in range(3)], axis=1)
     vol_mat[...] = triple(kron(vol_held, stiff, factors))
-
-    first_part, late_part = predict(x_ref[...], [(0.0, STEP), (STEP, 2.0 * STEP)])
-
-    eye = onehot(iota((SLOTS, SLOTS), 0) == iota((SLOTS, SLOTS), 1))
-    named = nt(eye, snd_in[...].astype(F32).astype(BF16))
-    elem = iota((SLOTS, ELEMS), 1)
-    picks = jnp.concatenate(
-        [onehot(named[:, d : d + 1].astype(jnp.int32) == elem) for d in range(4)], axis=0
-    )
-    pick_both = jnp.concatenate([picks, picks], axis=1)
-
-    outgoing[:, :, pl.ds(ROWS, LANES - ROWS)] = jnp.zeros((2, ELEMS, LANES - ROWS), F32)
-
-    def send(turn, values):
-        outgoing[turn, :, pl.ds(0, ROWS)] = nt(pick_both, wide(values))
-        if turn == 0:
-            pl.semaphore_wait(barrier, partners)
-        copies = []
-        for d in range(4):
-            part = pl.ds(SLOTS * d, SLOTS)
-            copy = pltpu.make_async_remote_copy(
-                src_ref=outgoing.at[turn, part],
-                dst_ref=ghosts.at[turn, part],
-                send_sem=send_sem.at[turn, d],
-                recv_sem=recv_sem.at[turn, d],
-                device_id=targets[d],
-                device_id_type=MESH,
-            )
-            pl.when(sends[d])(copy.start)
-            copies.append(copy)
-        return copies
-
-    copies_one = send(0, first_part)
 
     loads[9].wait()
     loads[10].wait()

time: 30.8 us -> 30.5 us (level)
    pallas_call x1, Pallas kernels: 30 us -> 29.7 us  [local(): pl.pallas_call(kernel, out_shape=pltpu.VMEM((QUANT, BASIS, ELEMS), F32),...]
where the time goes in v9:
time: 30.5 us; the launch traced here: 30.3 us
  Pallas kernels  29.7 us (97%)
  local copies, waits for them, and re-layouts  0.65 us (2%)
    pallas_call x1, Pallas kernels, local(): pl.pallas_call(kernel, out_shape=pltpu.VMEM((QUANT, BASIS, ELEMS), F32),...  29.7 us
    unnamed x1, local copies, waits for them, and re-layouts  0.65 us

profile of v9, /device:TPU:30, one launch (start us, length us, event | category | flops | bytes accessed | tf_op | source)
XLA Modules:
  0.0 30.3 jit_solution(12963242742290692371)
XLA Ops:
  0.0 29.7 %shard_map.136 = f32[9,20,128]{2,1,0:T(8,128)S(1)} custom-call(f32[9,20,128]{2,1,0:T(8,128)} %bitcast.10, f32[7,128]{1,0:T(8,128)} %geo_any.1, s32[1,128]{1,0:T(1,128)} %bitcast.17, s32[4,128]{1,0:T(4,128)} %nb_any.1, s32[4,128]{1,0:T(4,128)} %ori_any.1, s32[4,32]{1,0:T(4,128)} %snd_any.1, f32[3,20,20]{2,1,0:T(8,128)} %st_any.1, f32[3,20,20]{2,1,0:T(8,128)} %sv_any.1, ...), custom_call_target="tpu_custom_call" | custom-call | tf_op jit(solution)/shard_map/pallas_call | solution.py:349
  29.7 0.6 %copy.16 = f32[20,9,128]{2,0,1:T(8,128)} copy(f32[20,9,128]{2,0,1:T(8,128)S(1)} %bitcast.9) | data formatting | bytes 184320
